TPU v7x, 32 devices: a whole 2x2x4 slice. The times are simulated.
32 devices in a mesh: dp: 1, expert: 32 (over z, y, x, core).
Axes of the slice: x: 2, y: 2, z: 4, core: 2. Of those that a mesh axis runs over, the one named last changes fastest.
Arguments:
- queries: bfloat16 [1024, 4096], P('dp', 'expert'), may hold values from -140 to 140
- keys: bfloat16 [1024, 256], P(('dp', 'expert')), may hold values from -4 to 4
- values: bfloat16 [1024, 256], P(('dp', 'expert')), may hold values from -4 to 4
- span_ids: int32 [1024], P('dp'), may hold values from 0 to 9, as said below
- residual: bfloat16 [1024, 4096], P(('dp', 'expert')), may hold values from -6 to 6
- norm_gain: float32 [4096], replicated, may hold values from 0.1 to 1.9
- routes: int32 [1024, 8], P(('dp', 'expert')), may hold values from 0 to 127, as said below
- gates: float32 [1024, 8], P(('dp', 'expert')), may hold values from 0.2 to 1
- w_gate: bfloat16 [4096, 4096], P('expert'), may hold values from -0.09375 to 0.09375
- w_up: bfloat16 [4096, 4096], P('expert'), may hold values from -0.09375 to 0.09375
- w_down: bfloat16 [4096, 4096], P('expert'), may hold values from -0.1875 to 0.1875
Outputs:
- mixed: bfloat16 [1024, 4096], P(('dp', 'expert'))
Inputs may be any that keep to these rules, and one draw needn't show every extreme that they name: `span_ids`: span numbers start at 0 and never fall along the positions; every span starts at an even position, has 2 to 512 positions and never crosses a multiple of 512; one aligned block of 512 positions is a single span, and every other holds exactly 9 spans. `routes`: each row names 8 different experts. In the rows of one device (aligned blocks of 32 rows) each expert below 4 is named by at most 8 rows, and exactly one such expert, changing from block to block, by exactly 8 rows; every expert below 4 is that one in some block.
All inputs are finite; a program needn't handle non-finite values.
Results may differ from a plain program's by a relative error of at most 0.0054.
Values may be sent and summed in bfloat16 or wider, within the bound.
A program may use at most 64 MiB of HBM per device.

v0:
```python
import math

import jax
import jax.numpy as jnp
from jax import lax
from jax.sharding import PartitionSpec as P

KV_HEADS = 4
HEAD_DIM = 64
FF_WIN = 1024
SPAN = 512


def from_partner(value, axis, distance):
    mask = 2**distance
    pairs = [(source, source ^ mask) for source in range(lax.axis_size(axis))]
    return lax.ppermute(value, axis, pairs)


def attend(queries, key_mine, value_mine, span_ids):
    tokens_all, head_width = queries.shape
    heads_here = head_width // HEAD_DIM
    blocks = tokens_all // SPAN
    score_scale = 1.0 / math.sqrt(HEAD_DIM)
    positions = jnp.arange(SPAN)
    causal = positions[None, :] <= positions[:, None]

    def one_block(pieces):
        query_blk, key_blk, value_blk, ids_blk = pieces
        scores = (
            jnp.einsum("qhd,kd->hqk", query_blk, key_blk, preferred_element_type=jnp.float32)
            * score_scale
        )
        allowed = causal & (ids_blk[None, :] == ids_blk[:, None])
        scores = jnp.where(allowed[None], scores, -jnp.inf)
        highest = jnp.max(scores, axis=-1, keepdims=True)
        raised = jnp.exp(scores - highest)
        attn_weights = (raised / jnp.sum(raised, axis=-1, keepdims=True)).astype(jnp.bfloat16)
        attended_blk = jnp.einsum(
            "hqk,kd->qhd", attn_weights, value_blk, preferred_element_type=jnp.float32
        )
        return attended_blk.astype(jnp.bfloat16)

    result = lax.map(
        one_block,
        (
            queries.reshape(blocks, SPAN, heads_here, HEAD_DIM),
            key_mine.reshape(blocks, SPAN, HEAD_DIM),
            value_mine.reshape(blocks, SPAN, HEAD_DIM),
            span_ids.reshape(blocks, SPAN),
        ),
    )
    return result.reshape(tokens_all, head_width)


def shards(
    queries, keys, values, span_ids, residual, norm_gain, routes, gates, w_gate, w_up, w_down
):
    devices = lax.axis_size("expert")
    my_index = lax.axis_index("expert")
    tok_local = residual.shape[0]
    joined = jnp.concatenate(
        [
            keys.reshape(tok_local, KV_HEADS, HEAD_DIM),
            values.reshape(tok_local, KV_HEADS, HEAD_DIM),
        ],
        axis=2,
    )
    spread = jnp.repeat(joined, devices // KV_HEADS, axis=1)
    arrived_heads = lax.all_to_all(spread, "expert", split_axis=1, concat_axis=0, tiled=True)
    key_mine = arrived_heads[:, 0, :HEAD_DIM]
    value_mine = arrived_heads[:, 0, HEAD_DIM:]
    attended_heads = attend(queries, key_mine, value_mine, span_ids)
    attended = lax.all_to_all(attended_heads, "expert", split_axis=0, concat_axis=1, tiled=True)
    stream_wide = residual.astype(jnp.float32) + attended.astype(jnp.float32)
    stream = stream_wide.astype(jnp.bfloat16)
    stream_wide = stream.astype(jnp.float32)
    inverse = lax.rsqrt(jnp.mean(stream_wide * stream_wide, axis=-1, keepdims=True) + 1e-06)
    normed = (stream_wide * inverse * norm_gain).astype(jnp.bfloat16)
    group = FF_WIN // w_gate.shape[0]
    group_bits = group.bit_length() - 1
    wave = devices // group
    capacity = tok_local // 4
    slot_count = capacity // group
    model_width = normed.shape[1]
    expert_ids = jnp.arange(wave, dtype=jnp.int32)
    hits = routes[:, :, None] == expert_ids[None, None, :]
    named = jnp.any(hits, axis=1)
    weight = jnp.sum(jnp.where(hits, gates[:, :, None], 0.0), axis=1)
    slot_index = jnp.cumsum(named.astype(jnp.int32), axis=0) - 1
    selector = named.T[:, None, :] & (
        slot_index.T[:, None, :] == jnp.arange(capacity)[None, :, None]
    )
    outgoing = jnp.einsum(
        "ect,td->ecd", selector.astype(jnp.bfloat16), normed, preferred_element_type=jnp.float32
    ).astype(jnp.bfloat16)
    outgoing = outgoing.reshape(devices, slot_count, model_width)
    gathered = lax.all_to_all(outgoing, "expert", split_axis=0, concat_axis=0, tiled=True)
    for bit_number in range(group_bits):
        partner = from_partner(gathered, "expert", bit_number)
        lower = my_index // 2**bit_number % 2 == 0
        gathered = jnp.where(
            lower,
            jnp.concatenate([gathered, partner], axis=1),
            jnp.concatenate([partner, gathered], axis=1),
        )
    token_rows = gathered.reshape(devices * capacity, model_width)
    dims = (((1,), (1,)), ((), ()))
    gate_pre = lax.dot_general(token_rows, w_gate, dims, preferred_element_type=jnp.float32)
    up_pre = lax.dot_general(token_rows, w_up, dims, preferred_element_type=jnp.float32)
    hidden = (jax.nn.silu(gate_pre) * up_pre).astype(jnp.bfloat16)
    piece = jnp.dot(hidden, w_down, preferred_element_type=jnp.float32).astype(jnp.bfloat16)
    piece = piece.reshape(devices, capacity, model_width)
    returned = lax.all_to_all(piece, "expert", split_axis=0, concat_axis=0, tiled=True)
    expert_out = jnp.sum(
        returned.reshape(wave, group, capacity, model_width).astype(jnp.float32), axis=1
    )
    flat_slots = expert_ids[None, :] * capacity + jnp.maximum(slot_index, 0)
    picked = jnp.take(
        expert_out.reshape(wave * capacity, model_width), flat_slots.reshape(-1), axis=0
    )
    picked = picked.reshape(tok_local, wave, model_width)
    combined = jnp.sum(weight[:, :, None] * picked, axis=1)
    return (stream_wide + combined).astype(jnp.bfloat16)


def solution(mesh):
    return jax.shard_map(
        shards,
        mesh=mesh,
        in_specs=(
            P("dp", "expert"),
            P(("dp", "expert"), None),
            P(("dp", "expert"), None),
            P("dp"),
            P(("dp", "expert"), None),
            P(),
            P(("dp", "expert"), None),
            P(("dp", "expert"), None),
            P("expert", None),
            P("expert", None),
            P("expert", None),
        ),
        out_specs=P(("dp", "expert"), None),
        check_vma=False,
    )
```

profile of v0, /device:TPU:0, one launch (start us, length us, event | category | flops | bytes accessed | tf_op | source)
XLA Modules:
  0.0 171.7 jit_solution(3322995648816507542)
XLA Ops:
  0.0 0.9 reshape.148
  0.9 0.8 reshape.149
  1.7 0.1 pad_maximum_fusion
  1.8 0.7 broadcast_in_dim.62
  2.6 7.3 %all-to-all-start = ((bf16[32,32,128]{2,0,1:T(8,128)(2,1)}), bf16[32,32,128]{2,0,1:T(8,128)(2,1)S(1)}, u32[]{:S(2)}, u32[]{:S(2)}) async-start(bf16[32,32,128]{2,0,1:T(8,128)(2,1)} %bitcast), calls=%async_computation | async-start | bytes 524288 | tf_op jit(solution)/shard_map/all_to_all | solution.py:70
  9.9 1.2 reshape.169
  11.1 0.4 copy.67
  11.5 9.0 %all-to-all-done = bf16[32,32,128]{2,0,1:T(8,128)(2,1)S(1)} async-done(((bf16[32,32,128]{2,0,1:T(8,128)(2,1)}), bf16[32,32,128]{2,0,1:T(8,128)(2,1)S(1)}, u32[]{:S(2)}, u32[]{:S(2)}) %all-to-all-start) | async-done | bytes 262176 | tf_op jit(solution)/shard_map/all_to_all | solution.py:70
  20.5 0.1 fusion.86
  20.6 0.1 copy.65
  20.8 0.1 copy.66
  20.9 4.6 %while.11 = (s32[]{:T(128)}, bf16[2,512,2,64]{1,3,2,0:T(8,128)(2,1)S(1)}, bf16[2,512,64]{1,2,0:T(8,128)(2,1)S(1)}, s32[2,512]{1,0:T(2,128)S(1)}, bf16[2,512,64]{...) while((s32[]{:T(128)}, bf16[2,512,2,64]{1,3,2,0:T(8,128)(2,1)S(1)}, ...), condition=%wide.region_3.4_spmd.clone, body=%wide.region_0.3_spmd.clone.sunk | while | flops 206899200 | bytes 1393745 | solution.py:44
  20.9 0.2 fusion.103
  21.1 0.9 fusion.104
  22.1 1.1 fusion.105
  23.2 0.2 fusion.103
  23.5 0.9 fusion.104
  24.4 1.1 fusion.105
  25.6 0.4 copy.68
  26.0 1.0 all_to_all.33
  27.0 2.6 %all-to-all-start.1 = ((bf16[32,32,128]{2,1,0:T(8,128)(2,1)}), bf16[32,32,128]{2,1,0:T(8,128)(2,1)S(1)}, u32[]{:S(2)}, u32[]{:S(2)}) async-start(bf16[32,32,128]{2,1,0:T(8,128)(2,1)} %all_to_all.33), calls=%async_computation.1 | async-start | bytes 524288 | tf_op jit(solution)/shard_map/all_to_all | solution.py:74
  29.8 10.3 %all-to-all-done.1 = bf16[32,32,128]{2,1,0:T(8,128)(2,1)S(1)} async-done(((bf16[32,32,128]{2,1,0:T(8,128)(2,1)}), bf16[32,32,128]{2,1,0:T(8,128)(2,1)S(1)}, u32[]{:S(2)}, u32[]{:S(2)}) %all-to-all-start.1) | async-done | bytes 262176 | tf_op jit(solution)/shard_map/all_to_all | solution.py:74
  40.2 0.2 fusion.52
  40.4 0.3 fusion.50
  40.7 0.5 broadcast.148
  41.2 0.8 reduce
  42.0 0.2 reshape.170
  42.2 12.7 %all_to_all.41 = bf16[32,2,2048]{2,1,0:T(2,128)(2,1)S(1)} all-to-all(bf16[32,2,2048]{2,1,0:T(2,128)(2,1)S(1)} %reshape.170), channel_id=1, replica_groups=mesh['dp'=1,'expert'=32] {'expert'}, dimensions={0} | all-to-all | bytes 524288 | tf_op jit(solution)/shard_map/all_to_all | solution.py:98
  54.9 0.3 reshape.171
  55.2 1.9 %collective-permute-done = bf16[32,1,4096]{2,1,0:T(2,128)(2,1)S(1)} collective-permute-done((bf16[32,1,4096]{2,1,0:T(2,128)(2,1)S(1)}, bf16[32,1,4096]{2,1,0:T(2,128)(2,1)S(1)}, u32[]{:S(2)}, u32[]{:S(2)}) %collective-permute-start) | collective-permute-done | bytes 262176 | tf_op jit(solution)/shard_map/ppermute | solution.py:17
  57.1 2.3 %broadcast_select_fusion = bf16[32,2,4096]{2,1,0:T(2,128)(2,1)S(1)} fusion(pred[]{:T(512)S(6)} %eq.61, bf16[32,1,4096]{2,1,0:T(2,128)(2,1)S(1)} %collective-permute-done, bf16[32,1,4096]{2,1,0:T(2,128)(2,1)S(1)} %reshape.171), kind=kLoop, calls=%fused_computation.44 | loop fusion | flops 2359296 | bytes 1048577 | tf_op jit(solution)/shard_map/jit(_where)/select_n | solution.py:102
  59.5 0.5 collective-permute-start.1
  60.0 13.5 %collective-permute-done.1 = bf16[32,2,4096]{2,1,0:T(2,128)(2,1)S(1)} collective-permute-done((bf16[32,2,4096]{2,1,0:T(2,128)(2,1)S(1)}, bf16[32,2,4096]{2,1,0:T(2,128)(2,1)S(1)}, u32[]{:S(2)}, u32[]{:S(2)}) %collective-permute-start.1) | collective-permute-done | bytes 524320 | tf_op jit(solution)/shard_map/ppermute | solution.py:17
  73.5 1.9 %maximum_select_fusion.1 = bf16[32,4,4096]{2,1,0:T(4,128)(2,1)S(1)} fusion(bf16[32,2,4096]{2,1,0:T(2,128)(2,1)S(1)} %collective-permute-done.1, bf16[32,2,4096]{2,1,0:T(2,128)(2,1)S(1)} %broadcast_select_fusion, pred[]{:T(512)S(6)} %eq.60), kind=kLoop, calls=%fused_computation.43 | loop fusion | flops 4718592 | bytes 2097153 | tf_op jit(solution)/shard_map/jit(_where)/select_n | solution.py:102
  75.4 1.0 collective-permute-start.2
  76.3 23.6 %collective-permute-done.2 = bf16[32,4,4096]{2,1,0:T(4,128)(2,1)} collective-permute-done((bf16[32,4,4096]{2,1,0:T(4,128)(2,1)S(1)}, bf16[32,4,4096]{2,1,0:T(4,128)(2,1)}, u32[]{:S(2)}, u32[]{:S(2)}) %collective-permute-start.2) | collective-permute-done | bytes 1048608 | tf_op jit(solution)/shard_map/ppermute | solution.py:17
  99.9 4.0 %fusion.57 = f32[256,128]{1,0:T(8,128)S(1)} fusion(bf16[128,4096]{1,0:T(8,128)(2,1)} %param.22, bf16[32,4,4096]{2,1,0:T(4,128)(2,1)} %collective-permute-done.2, bf16[32,4,4096]{2,1,0:T(4,128)(2,1)S(1)} %maximum_select_fusion.1, pred[]{:T(512)S(6)} %eq.59), kind=kOutput, calls=%fused_computation.55 | convolution fusion | flops 277872640 | bytes 3276801 | tf_op jit(solution)/shard_map/dot_general | solution.py:110
  103.9 6.2 %fusion.49 = bf16[32,8,4096]{2,1,0:T(8,128)(2,1)} fusion(bf16[128,4096]{1,0:T(8,128)(2,1)S(1)} %copy-done, f32[256,128]{1,0:T(8,128)S(1)} %fusion.57, bf16[128,4096]{1,0:T(8,128)(2,1)S(1)} %copy-done.6, bf16[32,4,4096]{2,1,0:T(4,128)(2,1)} %collective-permute-done.2, bf16[32,4,4096]{2,1,0:T(4,128)(2,1)S(1)} %maximum_select_fusion.1, pred[]{:T(512)S(6)} %eq.59), kind=kOutput, calls=%fused_computation.36 | convolution fusion | flops 547553280 | bytes 6422529 | tf_op jit(solution)/shard_map/dot_general | solution.py:112
  110.1 3.8 %all-to-all-start.3 = ((bf16[32,8,4096]{2,1,0:T(8,128)(2,1)}), bf16[32,8,4096]{2,1,0:T(8,128)(2,1)}, u32[]{:S(2)}, u32[]{:S(2)}) async-start(bf16[32,8,4096]{2,1,0:T(8,128)(2,1)} %fusion.49), calls=%async_computation.3 | async-start | bytes 4194304 | tf_op jit(solution)/shard_map/all_to_all | solution.py:114
  114.1 0.1 add.107
  114.2 0.1 copy.73
  114.4 0.1 copy.70
  114.5 48.4 %all-to-all-done.3 = bf16[32,8,4096]{2,1,0:T(8,128)(2,1)} async-done(((bf16[32,8,4096]{2,1,0:T(8,128)(2,1)}), bf16[32,8,4096]{2,1,0:T(8,128)(2,1)}, u32[]{:S(2)}, u32[]{:S(2)}) %all-to-all-start.3) | async-done | bytes 2097184 | tf_op jit(solution)/shard_map/all_to_all | solution.py:114
  162.9 2.0 %convert_reduce_fusion = f32[4,8,4096]{2,1,0:T(8,128)S(1)} fusion(bf16[32,8,4096]{2,1,0:T(8,128)(2,1)} %all-to-all-done.3), kind=kLoop, calls=%fused_computation.39 | loop fusion | flops 1966080 | bytes 2621440 | tf_op jit(solution)/shard_map/reduce_sum | solution.py:115
  164.8 2.6 %gather_fusion = f32[128,4096]{1,0:T(8,128)} fusion(f32[32,4096]{1,0:T(8,128)S(1)} %bitcast.111, s32[1024]{0:T(1024)S(1)} %pad_clamp_fusion), kind=kCustom, calls=%fused_computation | custom fusion | bytes 4194816 | tf_op jit(solution)/shard_map/jit(_take)/gather | solution.py:119
  167.4 1.9 %gather.7 = f32[32,4,4096]{2,1,0:T(4,128)S(1)} reshape(f32[128,4096]{1,0:T(8,128)} %gather_fusion) | data formatting | bytes 4194304 | tf_op jit(solution)/shard_map/jit(_take)/gather | solution.py:119
  169.3 1.7 multiply_reduce_fusion
  170.9 0.8 fusion.55
  (33 shorter events, 0.6 us)
Async XLA Ops:
  0.0 103.9 %copy-start = (bf16[128,4096]{1,0:T(8,128)(2,1)S(1)}, bf16[128,4096]{1,0:T(8,128)(2,1)}, u32[]{:S(2)}) copy-start(bf16[128,4096]{1,0:T(8,128)(2,1)} %param.23) | copy-start | bytes 3145732
  0.0 11.5 %copy-start.4 = (s32[1024]{0:T(1024)S(1)}, s32[1024]{0:T(1024)}, u32[]{:S(2)}) copy-start(s32[1024]{0:T(1024)} %param.16) | copy-start | bytes 12292
  2.6 17.9 %all-to-all-start = ((bf16[32,32,128]{2,0,1:T(8,128)(2,1)}), bf16[32,32,128]{2,0,1:T(8,128)(2,1)S(1)}, u32[]{:S(2)}, u32[]{:S(2)}) async-start(bf16[32,32,128]{2,0,1:T(8,128)(2,1)} %bitcast), calls=%async_computation | async-start | bytes 524288 | tf_op jit(solution)/shard_map/all_to_all | solution.py:70
  25.5 4.0 %copy-start.3 = (s32[32,8]{0,1:T(8,128)S(1)}, s32[32,8]{0,1:T(8,128)}, u32[]{:S(2)}) copy-start(s32[32,8]{0,1:T(8,128)} %param.19) | copy-start | bytes 3076
  25.6 14.6 %copy-start.1 = (bf16[32,4096]{1,0:T(8,128)(2,1)S(1)}, bf16[32,4096]{1,0:T(8,128)(2,1)}, u32[]{:S(2)}) copy-start(bf16[32,4096]{1,0:T(8,128)(2,1)} %param.17) | copy-start | bytes 786436
  25.6 14.8 %copy-start.2 = (f32[4096]{0:T(1024)S(1)}, f32[4096]{0:T(1024)}, u32[]{:S(2)}) copy-start(f32[4096]{0:T(1024)} %param.18) | copy-start | bytes 49156
  27.0 13.2 %all-to-all-start.1 = ((bf16[32,32,128]{2,1,0:T(8,128)(2,1)}), bf16[32,32,128]{2,1,0:T(8,128)(2,1)S(1)}, u32[]{:S(2)}, u32[]{:S(2)}) async-start(bf16[32,32,128]{2,1,0:T(8,128)(2,1)} %all_to_all.33), calls=%async_computation.1 | async-start | bytes 524288 | tf_op jit(solution)/shard_map/all_to_all | solution.py:74
  55.1 2.0 %collective-permute-start = (bf16[32,1,4096]{2,1,0:T(2,128)(2,1)S(1)}, bf16[32,1,4096]{2,1,0:T(2,128)(2,1)S(1)}, u32[]{:S(2)}, u32[]{:S(2)}) collective-permute-start(bf16[32,1,4096]{2,1,0:T(2,128)(2,1)S(1)} %reshape.171), channel_id=1, source_target_pairs={{0,1},{1,0},{2,3},{3,2},{4,5},{5,4},{6,7},{7,6},{8,9},{9,8},{10,11... | collective-permute-start | bytes 786440 | tf_op jit(solution)/shard_map/ppermute | solution.py:17
  59.5 14.0 %collective-permute-start.1 = (bf16[32,2,4096]{2,1,0:T(2,128)(2,1)S(1)}, bf16[32,2,4096]{2,1,0:T(2,128)(2,1)S(1)}, u32[]{:S(2)}, u32[]{:S(2)}) collective-permute-start(bf16[32,2,4096]{2,1,0:T(2,128)(2,1)S(1)} %broadcast_select_fusion), channel_id=1, source_target_pairs={{0,2},{1,3},{2,0},{3,1},{4,6},{5,7},{6,4},{7,5},{8,10},{9,11},{10,... | collective-permute-start | bytes 1572872 | tf_op jit(solution)/shard_map/ppermute | solution.py:17
  75.4 24.5 %collective-permute-start.2 = (bf16[32,4,4096]{2,1,0:T(4,128)(2,1)S(1)}, bf16[32,4,4096]{2,1,0:T(4,128)(2,1)}, u32[]{:S(2)}, u32[]{:S(2)}) collective-permute-start(bf16[32,4,4096]{2,1,0:T(4,128)(2,1)S(1)} %maximum_select_fusion.1), channel_id=1, source_target_pairs={{0,4},{1,5},{2,6},{3,7},{4,0},{5,1},{6,2},{7,3},{8,12},{9,13},{10,... | collective-permute-start | bytes 3145736 | tf_op jit(solution)/shard_map/ppermute | solution.py:17
  76.3 27.6 %copy-start.6 = (bf16[128,4096]{1,0:T(8,128)(2,1)S(1)}, bf16[128,4096]{1,0:T(8,128)(2,1)}, u32[]{:S(2)}) copy-start(bf16[128,4096]{1,0:T(8,128)(2,1)} %param.21) | copy-start | bytes 3145732
  110.1 4.2 %copy-start.5 = (f32[32,8]{0,1:T(8,128)S(1)}, f32[32,8]{0,1:T(8,128)}, u32[]{:S(2)}) copy-start(f32[32,8]{0,1:T(8,128)} %param.20) | copy-start | bytes 3076
  110.1 52.7 %all-to-all-start.3 = ((bf16[32,8,4096]{2,1,0:T(8,128)(2,1)}), bf16[32,8,4096]{2,1,0:T(8,128)(2,1)}, u32[]{:S(2)}, u32[]{:S(2)}) async-start(bf16[32,8,4096]{2,1,0:T(8,128)(2,1)} %fusion.49), calls=%async_computation.3 | async-start | bytes 4194304 | tf_op jit(solution)/shard_map/all_to_all | solution.py:114
where the time goes:
time: 172 us
  waiting for transfers between devices  107 us (62%)
  starting transfers between devices  15.3 us (9%)
  matrix products  14.6 us (8%)
  blocking collectives  12.7 us (7%)
  local copies, waits for them, and re-layouts  11.8 us (7%)
  other arithmetic  10.4 us (6%)
    all_to_all x1, waiting for transfers between devices, shards(): lax.all_to_all(piece, 'expert', split_axis=0, concat_axis=0, tiled=True)  48.4 us
    ppermute x3, waiting for transfers between devices, from_partner(): return lax.ppermute(value, axis, pairs)  39 us
    all_to_all x1, blocking collectives, shards(): lax.all_to_all(outgoing, 'expert', split_axis=0, concat_axis=0, tiled=True)  12.7 us
    all_to_all x1, waiting for transfers between devices, shards(): lax.all_to_all(attended_heads, 'expert', split_axis=0, concat_axis=1, til...  10.3 us
    all_to_all x1, waiting for transfers between devices, shards(): lax.all_to_all(spread, 'expert', split_axis=1, concat_axis=0, tiled=True)  8.96 us
    all_to_all x1, starting transfers between devices, shards(): lax.all_to_all(spread, 'expert', split_axis=1, concat_axis=0, tiled=True)  7.3 us
    dot_general x1, matrix products, shards(): jnp.dot(hidden, w_down, preferred_element_type=jnp.float32)  6.19 us
    gather x2, local copies, waits for them, and re-layouts, shards(): jnp.take(expert_out.reshape(wave * capacity, model_width), flat_slots.res...  4.43 us
  transfers between devices with their start and end apart: 6, of which 6 were waited for; matrix products, arithmetic and copies ran while one was open for 1% of the time, Pallas kernels for 0%

commit v1 on v0

--- a/solution.py
+++ b/solution.py
@@ -87,7 +87,8 @@
     hits = routes[:, :, None] == expert_ids[None, None, :]
     named = jnp.any(hits, axis=1)
     weight = jnp.sum(jnp.where(hits, gates[:, :, None], 0.0), axis=1)
-    slot_index = jnp.cumsum(named.astype(jnp.int32), axis=0) - 1
+    ahead = jnp.arange(tok_local)[None, :, None] <= jnp.arange(tok_local)[:, None, None]
+    slot_index = jnp.sum((ahead & named[None, :, :]).astype(jnp.int32), axis=1) - 1
     selector = named.T[:, None, :] & (
         slot_index.T[:, None, :] == jnp.arange(capacity)[None, :, None]
     )

time: 172 us -> 173 us (level)
  no operation moved by 1% of the time
where the time goes in v1:
time: 173 us; the launch traced here: 172 us
  waiting for transfers between devices  107 us (62%)
  starting transfers between devices  15.3 us (9%)
  matrix products  14.9 us (9%)
  blocking collectives  12.7 us (7%)
  local copies, waits for them, and re-layouts  11.7 us (7%)
  other arithmetic  10.5 us (6%)
    all_to_all x1, waiting for transfers between devices, shards(): lax.all_to_all(piece, 'expert', split_axis=0, concat_axis=0, tiled=True)  48.4 us
    ppermute x3, waiting for transfers between devices, from_partner(): return lax.ppermute(value, axis, pairs)  39 us
    all_to_all x1, blocking collectives, shards(): lax.all_to_all(outgoing, 'expert', split_axis=0, concat_axis=0, tiled=True)  12.7 us
    all_to_all x1, waiting for transfers between devices, shards(): lax.all_to_all(attended_heads, 'expert', split_axis=0, concat_axis=1, til...  10.4 us
    all_to_all x1, waiting for transfers between devices, shards(): lax.all_to_all(spread, 'expert', split_axis=1, concat_axis=0, tiled=True)  8.97 us
    all_to_all x1, starting transfers between devices, shards(): lax.all_to_all(spread, 'expert', split_axis=1, concat_axis=0, tiled=True)  7.3 us
    dot_general x1, matrix products, shards(): jnp.dot(hidden, w_down, preferred_element_type=jnp.float32)  6.39 us
    gather x2, local copies, waits for them, and re-layouts, shards(): jnp.take(expert_out.reshape(wave * capacity, model_width), flat_slots.res...  4.43 us
  transfers between devices with their start and end apart: 6, of which 6 were waited for; matrix products, arithmetic and copies ran while one was open for 1% of the time, Pallas kernels for 0%

profile of v1, /device:TPU:0, one launch (start us, length us, event | category | flops | bytes accessed | tf_op | source)
XLA Modules:
  0.0 172.0 jit_solution(5058316305987026423)
XLA Ops:
  0.0 0.9 reshape.164
  0.9 0.8 reshape.165
  1.7 0.1 pad_maximum_fusion
  1.8 0.7 broadcast_in_dim.45
  2.6 7.3 %all-to-all-start = ((bf16[32,32,128]{2,0,1:T(8,128)(2,1)}), bf16[32,32,128]{2,0,1:T(8,128)(2,1)S(1)}, u32[]{:S(2)}, u32[]{:S(2)}) async-start(bf16[32,32,128]{2,0,1:T(8,128)(2,1)} %bitcast), calls=%async_computation | async-start | bytes 524288 | tf_op jit(solution)/shard_map/all_to_all | solution.py:70
  9.9 1.2 reshape.185
  11.1 0.4 copy.53
  11.5 9.0 %all-to-all-done = bf16[32,32,128]{2,0,1:T(8,128)(2,1)S(1)} async-done(((bf16[32,32,128]{2,0,1:T(8,128)(2,1)}), bf16[32,32,128]{2,0,1:T(8,128)(2,1)S(1)}, u32[]{:S(2)}, u32[]{:S(2)}) %all-to-all-start) | async-done | bytes 262176 | tf_op jit(solution)/shard_map/all_to_all | solution.py:70
  20.5 0.1 fusion.86
  20.6 0.1 copy.51
  20.8 0.1 copy.52
  20.9 4.6 %while.11 = (s32[]{:T(128)}, bf16[2,512,2,64]{1,3,2,0:T(8,128)(2,1)S(1)}, bf16[2,512,64]{1,2,0:T(8,128)(2,1)S(1)}, s32[2,512]{1,0:T(2,128)S(1)}, bf16[2,512,64]{...) while((s32[]{:T(128)}, bf16[2,512,2,64]{1,3,2,0:T(8,128)(2,1)S(1)}, ...), condition=%wide.region_3.4_spmd.clone, body=%wide.region_0.3_spmd.clone.sunk | while | flops 206899200 | bytes 1393745 | solution.py:44
  20.9 0.2 fusion.103
  21.2 0.9 fusion.104
  22.1 1.1 fusion.105
  23.2 0.2 fusion.103
  23.4 0.9 fusion.104
  24.4 1.1 fusion.105
  25.5 0.4 copy.54
  25.9 1.0 all_to_all.33
  26.9 2.6 %all-to-all-start.1 = ((bf16[32,32,128]{2,1,0:T(8,128)(2,1)}), bf16[32,32,128]{2,1,0:T(8,128)(2,1)S(1)}, u32[]{:S(2)}, u32[]{:S(2)}) async-start(bf16[32,32,128]{2,1,0:T(8,128)(2,1)} %all_to_all.33), calls=%async_computation.1 | async-start | bytes 524288 | tf_op jit(solution)/shard_map/all_to_all | solution.py:74
  29.6 0.2 convert_reduce_fusion.1
  29.7 10.4 %all-to-all-done.1 = bf16[32,32,128]{2,1,0:T(8,128)(2,1)S(1)} async-done(((bf16[32,32,128]{2,1,0:T(8,128)(2,1)}), bf16[32,32,128]{2,1,0:T(8,128)(2,1)S(1)}, u32[]{:S(2)}, u32[]{:S(2)}) %all-to-all-start.1) | async-done | bytes 262176 | tf_op jit(solution)/shard_map/all_to_all | solution.py:74
  40.1 0.2 fusion.52
  40.4 0.3 fusion.50
  40.6 0.5 broadcast.158
  41.2 0.8 reduce
  41.9 0.2 reshape.186
  42.1 12.7 %all_to_all.41 = bf16[32,2,2048]{2,1,0:T(2,128)(2,1)S(1)} all-to-all(bf16[32,2,2048]{2,1,0:T(2,128)(2,1)S(1)} %reshape.186), channel_id=1, replica_groups=mesh['dp'=1,'expert'=32] {'expert'}, dimensions={0} | all-to-all | bytes 524288 | tf_op jit(solution)/shard_map/all_to_all | solution.py:99
  54.8 0.3 reshape.187
  55.2 1.9 %collective-permute-done = bf16[32,1,4096]{2,1,0:T(2,128)(2,1)S(1)} collective-permute-done((bf16[32,1,4096]{2,1,0:T(2,128)(2,1)S(1)}, bf16[32,1,4096]{2,1,0:T(2,128)(2,1)S(1)}, u32[]{:S(2)}, u32[]{:S(2)}) %collective-permute-start) | collective-permute-done | bytes 262176 | tf_op jit(solution)/shard_map/ppermute | solution.py:17
  57.1 2.3 %broadcast_select_fusion = bf16[32,2,4096]{2,1,0:T(2,128)(2,1)S(1)} fusion(pred[]{:T(512)S(6)} %eq.61, bf16[32,1,4096]{2,1,0:T(2,128)(2,1)S(1)} %collective-permute-done, bf16[32,1,4096]{2,1,0:T(2,128)(2,1)S(1)} %reshape.187), kind=kLoop, calls=%fused_computation.44 | loop fusion | flops 2359296 | bytes 1048577 | tf_op jit(solution)/shard_map/jit(_where)/select_n | solution.py:103
  59.4 0.5 collective-permute-start.1
  60.0 13.5 %collective-permute-done.1 = bf16[32,2,4096]{2,1,0:T(2,128)(2,1)S(1)} collective-permute-done((bf16[32,2,4096]{2,1,0:T(2,128)(2,1)S(1)}, bf16[32,2,4096]{2,1,0:T(2,128)(2,1)S(1)}, u32[]{:S(2)}, u32[]{:S(2)}) %collective-permute-start.1) | collective-permute-done | bytes 524320 | tf_op jit(solution)/shard_map/ppermute | solution.py:17
  73.5 1.9 %maximum_select_fusion.1 = bf16[32,4,4096]{2,1,0:T(4,128)(2,1)S(1)} fusion(bf16[32,2,4096]{2,1,0:T(2,128)(2,1)S(1)} %collective-permute-done.1, bf16[32,2,4096]{2,1,0:T(2,128)(2,1)S(1)} %broadcast_select_fusion, pred[]{:T(512)S(6)} %eq.60), kind=kLoop, calls=%fused_computation.43 | loop fusion | flops 4718592 | bytes 2097153 | tf_op jit(solution)/shard_map/jit(_where)/select_n | solution.py:103
  75.4 1.0 collective-permute-start.2
  76.3 23.6 %collective-permute-done.2 = bf16[32,4,4096]{2,1,0:T(4,128)(2,1)} collective-permute-done((bf16[32,4,4096]{2,1,0:T(4,128)(2,1)S(1)}, bf16[32,4,4096]{2,1,0:T(4,128)(2,1)}, u32[]{:S(2)}, u32[]{:S(2)}) %collective-permute-start.2) | collective-permute-done | bytes 1048608 | tf_op jit(solution)/shard_map/ppermute | solution.py:17
  99.9 4.1 %fusion.57 = f32[256,128]{1,0:T(8,128)S(1)} fusion(bf16[128,4096]{1,0:T(8,128)(2,1)} %param.22, bf16[32,4,4096]{2,1,0:T(4,128)(2,1)} %collective-permute-done.2, bf16[32,4,4096]{2,1,0:T(4,128)(2,1)S(1)} %maximum_select_fusion.1, pred[]{:T(512)S(6)} %eq.59), kind=kOutput, calls=%fused_computation.55 | convolution fusion | flops 277872640 | bytes 3276801 | tf_op jit(solution)/shard_map/dot_general | solution.py:111
  104.1 6.4 %fusion.49 = bf16[32,8,4096]{2,1,0:T(8,128)(2,1)} fusion(bf16[128,4096]{1,0:T(8,128)(2,1)S(1)} %copy-done, f32[256,128]{1,0:T(8,128)S(1)} %fusion.57, bf16[128,4096]{1,0:T(8,128)(2,1)S(1)} %copy-done.6, bf16[32,4,4096]{2,1,0:T(4,128)(2,1)} %collective-permute-done.2, bf16[32,4,4096]{2,1,0:T(4,128)(2,1)S(1)} %maximum_select_fusion.1, pred[]{:T(512)S(6)} %eq.59), kind=kOutput, calls=%fused_computation.36 | convolution fusion | flops 547553280 | bytes 6422529 | tf_op jit(solution)/shard_map/dot_general | solution.py:113
  110.5 3.8 %all-to-all-start.3 = ((bf16[32,8,4096]{2,1,0:T(8,128)(2,1)}), bf16[32,8,4096]{2,1,0:T(8,128)(2,1)}, u32[]{:S(2)}, u32[]{:S(2)}) async-start(bf16[32,8,4096]{2,1,0:T(8,128)(2,1)} %fusion.49), calls=%async_computation.3 | async-start | bytes 4194304 | tf_op jit(solution)/shard_map/all_to_all | solution.py:115
  114.5 0.1 add.107
  114.6 0.1 copy.57
  114.8 48.4 %all-to-all-done.3 = bf16[32,8,4096]{2,1,0:T(8,128)(2,1)} async-done(((bf16[32,8,4096]{2,1,0:T(8,128)(2,1)}), bf16[32,8,4096]{2,1,0:T(8,128)(2,1)}, u32[]{:S(2)}, u32[]{:S(2)}) %all-to-all-start.3) | async-done | bytes 2097184 | tf_op jit(solution)/shard_map/all_to_all | solution.py:115
  163.2 2.0 %convert_reduce_fusion = f32[4,8,4096]{2,1,0:T(8,128)S(1)} fusion(bf16[32,8,4096]{2,1,0:T(8,128)(2,1)} %all-to-all-done.3), kind=kLoop, calls=%fused_computation.39 | loop fusion | flops 1966080 | bytes 2621440 | tf_op jit(solution)/shard_map/reduce_sum | solution.py:116
  165.1 2.6 %gather_fusion = f32[128,4096]{1,0:T(8,128)} fusion(f32[32,4096]{1,0:T(8,128)S(1)} %bitcast.111, s32[1024]{0:T(1024)S(1)} %pad_clamp_fusion), kind=kCustom, calls=%fused_computation | custom fusion | bytes 4194816 | tf_op jit(solution)/shard_map/jit(_take)/gather | solution.py:120
  167.7 1.9 %gather.7 = f32[32,4,4096]{2,1,0:T(4,128)S(1)} reshape(f32[128,4096]{1,0:T(8,128)} %gather_fusion) | data formatting | bytes 4194304 | tf_op jit(solution)/shard_map/jit(_take)/gather | solution.py:120
  169.6 1.7 multiply_reduce_fusion
  171.3 0.8 fusion.55
  (31 shorter events, 0.5 us)
Async XLA Ops:
  0.0 104.0 %copy-start = (bf16[128,4096]{1,0:T(8,128)(2,1)S(1)}, bf16[128,4096]{1,0:T(8,128)(2,1)}, u32[]{:S(2)}) copy-start(bf16[128,4096]{1,0:T(8,128)(2,1)} %param.23) | copy-start | bytes 3145732
  0.0 11.5 %copy-start.4 = (s32[1024]{0:T(1024)S(1)}, s32[1024]{0:T(1024)}, u32[]{:S(2)}) copy-start(s32[1024]{0:T(1024)} %param.16) | copy-start | bytes 12292
  2.6 17.9 %all-to-all-start = ((bf16[32,32,128]{2,0,1:T(8,128)(2,1)}), bf16[32,32,128]{2,0,1:T(8,128)(2,1)S(1)}, u32[]{:S(2)}, u32[]{:S(2)}) async-start(bf16[32,32,128]{2,0,1:T(8,128)(2,1)} %bitcast), calls=%async_computation | async-start | bytes 524288 | tf_op jit(solution)/shard_map/all_to_all | solution.py:70
  25.5 4.0 %copy-start.3 = (s32[32,8]{0,1:T(8,128)S(1)}, s32[32,8]{0,1:T(8,128)}, u32[]{:S(2)}) copy-start(s32[32,8]{0,1:T(8,128)} %param.19) | copy-start | bytes 3076
  25.5 14.6 %copy-start.1 = (bf16[32,4096]{1,0:T(8,128)(2,1)S(1)}, bf16[32,4096]{1,0:T(8,128)(2,1)}, u32[]{:S(2)}) copy-start(bf16[32,4096]{1,0:T(8,128)(2,1)} %param.17) | copy-start | bytes 786436
  25.5 14.8 %copy-start.2 = (f32[4096]{0:T(1024)S(1)}, f32[4096]{0:T(1024)}, u32[]{:S(2)}) copy-start(f32[4096]{0:T(1024)} %param.18) | copy-start | bytes 49156
  26.9 13.2 %all-to-all-start.1 = ((bf16[32,32,128]{2,1,0:T(8,128)(2,1)}), bf16[32,32,128]{2,1,0:T(8,128)(2,1)S(1)}, u32[]{:S(2)}, u32[]{:S(2)}) async-start(bf16[32,32,128]{2,1,0:T(8,128)(2,1)} %all_to_all.33), calls=%async_computation.1 | async-start | bytes 524288 | tf_op jit(solution)/shard_map/all_to_all | solution.py:74
  55.1 2.0 %collective-permute-start = (bf16[32,1,4096]{2,1,0:T(2,128)(2,1)S(1)}, bf16[32,1,4096]{2,1,0:T(2,128)(2,1)S(1)}, u32[]{:S(2)}, u32[]{:S(2)}) collective-permute-start(bf16[32,1,4096]{2,1,0:T(2,128)(2,1)S(1)} %reshape.187), channel_id=1, source_target_pairs={{0,1},{1,0},{2,3},{3,2},{4,5},{5,4},{6,7},{7,6},{8,9},{9,8},{10,11... | collective-permute-start | bytes 786440 | tf_op jit(solution)/shard_map/ppermute | solution.py:17
  59.4 14.0 %collective-permute-start.1 = (bf16[32,2,4096]{2,1,0:T(2,128)(2,1)S(1)}, bf16[32,2,4096]{2,1,0:T(2,128)(2,1)S(1)}, u32[]{:S(2)}, u32[]{:S(2)}) collective-permute-start(bf16[32,2,4096]{2,1,0:T(2,128)(2,1)S(1)} %broadcast_select_fusion), channel_id=1, source_target_pairs={{0,2},{1,3},{2,0},{3,1},{4,6},{5,7},{6,4},{7,5},{8,10},{9,11},{10,... | collective-permute-start | bytes 1572872 | tf_op jit(solution)/shard_map/ppermute | solution.py:17
  75.4 24.5 %collective-permute-start.2 = (bf16[32,4,4096]{2,1,0:T(4,128)(2,1)S(1)}, bf16[32,4,4096]{2,1,0:T(4,128)(2,1)}, u32[]{:S(2)}, u32[]{:S(2)}) collective-permute-start(bf16[32,4,4096]{2,1,0:T(4,128)(2,1)S(1)} %maximum_select_fusion.1), channel_id=1, source_target_pairs={{0,4},{1,5},{2,6},{3,7},{4,0},{5,1},{6,2},{7,3},{8,12},{9,13},{10,... | collective-permute-start | bytes 3145736 | tf_op jit(solution)/shard_map/ppermute | solution.py:17
  76.3 27.7 %copy-start.6 = (bf16[128,4096]{1,0:T(8,128)(2,1)S(1)}, bf16[128,4096]{1,0:T(8,128)(2,1)}, u32[]{:S(2)}) copy-start(bf16[128,4096]{1,0:T(8,128)(2,1)} %param.21) | copy-start | bytes 3145732
  110.4 4.2 %copy-start.5 = (f32[32,8]{0,1:T(8,128)S(1)}, f32[32,8]{0,1:T(8,128)}, u32[]{:S(2)}) copy-start(f32[32,8]{0,1:T(8,128)} %param.20) | copy-start | bytes 3076
  110.5 52.7 %all-to-all-start.3 = ((bf16[32,8,4096]{2,1,0:T(8,128)(2,1)}), bf16[32,8,4096]{2,1,0:T(8,128)(2,1)}, u32[]{:S(2)}, u32[]{:S(2)}) async-start(bf16[32,8,4096]{2,1,0:T(8,128)(2,1)} %fusion.49), calls=%async_computation.3 | async-start | bytes 4194304 | tf_op jit(solution)/shard_map/all_to_all | solution.py:115

commit v2 on v0

v2 whole, which is shorter than its diff:
```python
import functools
import math

import jax
import jax.numpy as jnp
from jax import lax
from jax.experimental import pallas as pl
from jax.experimental.pallas import tpu as pltpu
from jax.sharding import PartitionSpec as P

KV_HEADS = 4
HEAD_DIM = 64
FF_WIN = 1024
SPAN = 512
MESH = pl.DeviceIdType.MESH
F32 = jnp.float32
BF16 = jnp.bfloat16


def remote(src, dst, send, recv, device):
    return pltpu.make_async_remote_copy(
        src_ref=src, dst_ref=dst, send_sem=send, recv_sem=recv,
        device_id={"expert": device}, device_id_type=MESH,
    )


def route_matrix(routes, gates, wave, capacity):
    tokens = routes.shape[0]
    columns = wave * capacity
    column = lax.broadcasted_iota(jnp.int32, (tokens, columns), 1)
    lower = (
        lax.broadcasted_iota(jnp.int32, (tokens, tokens), 0)
        >= lax.broadcasted_iota(jnp.int32, (tokens, tokens), 1)
    ).astype(F32)
    named_wide = jnp.zeros((tokens, columns), F32)
    weight_wide = jnp.zeros((tokens, columns), F32)
    for expert in range(wave):
        hits = routes == expert
        named = jnp.max(jnp.where(hits, 1.0, 0.0), axis=1, keepdims=True)
        weight = jnp.sum(jnp.where(hits, gates, 0.0), axis=1, keepdims=True)
        here = column // capacity == expert
        named_wide = jnp.where(here, named, named_wide)
        weight_wide = jnp.where(here, weight, weight_wide)
    count = jnp.dot(lower.astype(BF16), named_wide.astype(BF16), preferred_element_type=F32)
    slot = (column % capacity + 1).astype(F32)
    chosen = jnp.where(count == slot, named_wide, 0.0)
    return chosen, chosen * weight_wide


def moe_kernel(
    group, att, res, gain, routes, gates, wg, wu, wd, out,
    wgu_v, wd_v, outg, x_buf, part, core_buf, sums, plane_buf, final, back,
    w_sem, z_send, x_send, x_recv, c_send, c_recv, p_send, p_recv, b_send, b_recv,
):
    me = lax.axis_index("expert")
    wave = outg.shape[0]
    capacity = outg.shape[1] // 2
    tokens, width = res.shape
    half = width // 2
    hidden_here = wg.shape[0]
    mine = me % group
    plane = me // group
    base = plane * group

    def across(rz):
        return (plane ^ rz) * group + mine

    def within(r):
        return base + (mine ^ r)

    weights = [
        pltpu.make_async_copy(wg, wgu_v.at[pl.ds(0, hidden_here)], w_sem.at[0]),
        pltpu.make_async_copy(wu, wgu_v.at[pl.ds(hidden_here, hidden_here)], w_sem.at[1]),
        pltpu.make_async_copy(wd, wd_v, w_sem.at[2]),
    ]
    for copy in weights:
        copy.start()
    barrier = pltpu.get_barrier_semaphore()
    partners = [across(rz) for rz in range(1, wave)] + [within(r) for r in (1, 2, 4, 6)]
    for device in partners:
        pl.semaphore_signal(barrier, inc=1, device_id={"expert": device}, device_id_type=MESH)

    chosen, mix = route_matrix(routes[...], gates[...], wave, capacity)
    stream = (res[...].astype(F32) + att[...].astype(F32)).astype(BF16).astype(F32)
    inverse = lax.rsqrt(jnp.mean(stream * stream, axis=-1, keepdims=True) + 1e-06)
    normed = (stream * inverse * gain[...]).astype(BF16)
    rows = jnp.dot(chosen.T.astype(BF16), normed, preferred_element_type=F32)
    for expert in range(wave):
        block = rows[expert * capacity:(expert + 1) * capacity]
        outg[expert] = jnp.concatenate([block[:, :half], block[:, half:]], axis=0).astype(BF16)
    pl.semaphore_wait(barrier, len(partners))

    sends = []

    def go(copy):
        copy.start()
        sends.append(copy)
        return copy

    def arrived(ref, sem):
        pltpu.make_async_copy(ref, ref, sem).wait()

    for rz in range(1, wave):
        go(remote(outg.at[plane ^ rz], x_buf.at[0, rz], z_send.at[rz], x_recv.at[0, rz], across(rz)))
    x_buf[0, 0] = outg[plane]
    for rz in range(wave):
        if rz:
            arrived(x_buf.at[0, rz], x_recv.at[0, rz])
        for r in (2, 4, 6, 1):
            go(remote(x_buf.at[0, rz], x_buf.at[r, rz], x_send.at[r, rz], x_recv.at[r, rz], within(r)))
    for copy in weights:
        copy.wait()

    def fold(k):
        arrived(core_buf.at[k], c_recv.at[k])
        total = part[2 * k].astype(F32) + core_buf[k].astype(F32)
        sums[k] = total.astype(BF16)
        if k:
            go(remote(sums.at[k], plane_buf.at[k], p_send.at[k], p_recv.at[k], within(2 * k)))

    dims = (((1,), (1,)), ((), ()))
    pairs = group // 2
    for k in range(pairs):
        r = 2 * k
        if k:
            for rz in range(wave):
                arrived(x_buf.at[r, rz], x_recv.at[r, rz])
                go(remote(x_buf.at[r, rz], x_buf.at[r + 1, rz], x_send.at[r + 1, rz],
                          x_recv.at[r + 1, rz], within(1)))
        for rz in range(wave):
            arrived(x_buf.at[r + 1, rz], x_recv.at[r + 1, rz])
        x = x_buf[r:r + 2].reshape(2 * wave * 2 * capacity, half)
        left = lax.dot_general(x, wgu_v[:, :half], dims, preferred_element_type=F32)
        right = lax.dot_general(x, wgu_v[:, half:], dims, preferred_element_type=F32)
        left = left.reshape(2 * wave, 2 * capacity, 2 * hidden_here)[:, :capacity]
        right = right.reshape(2 * wave, 2 * capacity, 2 * hidden_here)[:, capacity:]
        pre = (left + right).reshape(2 * wave * capacity, 2 * hidden_here)
        gate_pre, up_pre = pre[:, :hidden_here], pre[:, hidden_here:]
        hidden = (gate_pre / (1.0 + jnp.exp(-gate_pre)) * up_pre).astype(BF16)
        piece = jnp.dot(hidden, wd_v[...], preferred_element_type=F32).astype(BF16)
        part[r] = piece[:wave * capacity]
        part[r + 1] = piece[wave * capacity:]
        go(remote(part.at[r + 1], core_buf.at[k], c_send.at[k], c_recv.at[k], within(1)))
        if k:
            fold(k - 1)
    fold(pairs - 1)

    total = sums[0].astype(F32)
    for k in range(1, pairs):
        arrived(plane_buf.at[k], p_recv.at[k])
        total = total + plane_buf[k].astype(F32)
    for rz in range(wave):
        block = total[rz * capacity:(rz + 1) * capacity]
        block = jnp.concatenate([block[:, :half], block[:, half:]], axis=0).astype(BF16)
        if rz:
            final[rz] = block
            go(remote(final.at[rz], back.at[plane], b_send.at[rz], b_recv.at[rz], across(rz)))
        else:
            back[plane] = block
    for rz in range(1, wave):
        arrived(back.at[plane ^ rz], b_recv.at[rz])

    high = mix.astype(BF16)
    rest = mix - high.astype(F32)
    middle = rest.astype(BF16)
    low = (rest - middle.astype(F32)).astype(BF16)
    outs = back[...].astype(F32)
    for side in range(2):
        columns = slice(side * half, (side + 1) * half)
        block = outs[:, side * capacity:(side + 1) * capacity].reshape(wave * capacity, half).astype(BF16)
        added = (
            jnp.dot(low, block, preferred_element_type=F32)
            + jnp.dot(middle, block, preferred_element_type=F32)
            + jnp.dot(high, block, preferred_element_type=F32)
        )
        out[:, columns] = (stream[:, columns] + added).astype(BF16)
    for copy in sends:
        copy.wait_send()


def experts(att, res, gain, routes, gates, wg, wu, wd):
    devices = lax.axis_size("expert")
    group = FF_WIN // wg.shape[0]
    wave = devices // group
    tokens, width = res.shape
    capacity = tokens // 4
    half = width // 2
    pairs = group // 2
    vmem = pl.BlockSpec(memory_space=pltpu.VMEM)
    hbm = pl.BlockSpec(memory_space=pl.ANY)
    dma = pltpu.SemaphoreType.DMA
    rows = wave * capacity
    return pl.pallas_call(
        functools.partial(moe_kernel, group),
        out_shape=jax.ShapeDtypeStruct((tokens, width), BF16),
        in_specs=[vmem] * 5 + [hbm] * 3,
        out_specs=vmem,
        scratch_shapes=[
            pltpu.VMEM((2 * wg.shape[0], width), BF16),
            pltpu.VMEM((wd.shape[0], width), BF16),
            pltpu.VMEM((wave, 2 * capacity, half), BF16),
            pltpu.VMEM((group, wave, 2 * capacity, half), BF16),
            pltpu.VMEM((group, rows, width), BF16),
            pltpu.VMEM((pairs, rows, width), BF16),
            pltpu.VMEM((pairs, rows, width), BF16),
            pltpu.VMEM((pairs, rows, width), BF16),
            pltpu.VMEM((wave, 2 * capacity, half), BF16),
            pltpu.VMEM((wave, 2 * capacity, half), BF16),
            dma((3,)), dma((wave,)), dma((group, wave)), dma((group, wave)),
            dma((pairs,)), dma((pairs,)), dma((pairs,)), dma((pairs,)), dma((wave,)), dma((wave,)),
        ],
        compiler_params=pltpu.CompilerParams(
            collective_id=0, has_side_effects=True, vmem_limit_bytes=48 * 2**20
        ),
    )(att, res, gain.reshape(1, width), routes, gates, wg, wu, wd)


def attend(queries, key_mine, value_mine, span_ids):
    tokens_all, head_width = queries.shape
    heads_here = head_width // HEAD_DIM
    blocks = tokens_all // SPAN
    score_scale = 1.0 / math.sqrt(HEAD_DIM)
    positions = jnp.arange(SPAN)
    causal = positions[None, :] <= positions[:, None]

    def one_block(pieces):
        query_blk, key_blk, value_blk, ids_blk = pieces
        scores = (
            jnp.einsum("qhd,kd->hqk", query_blk, key_blk, preferred_element_type=jnp.float32)
            * score_scale
        )
        allowed = causal & (ids_blk[None, :] == ids_blk[:, None])
        scores = jnp.where(allowed[None], scores, -jnp.inf)
        highest = jnp.max(scores, axis=-1, keepdims=True)
        raised = jnp.exp(scores - highest)
        attn_weights = (raised / jnp.sum(raised, axis=-1, keepdims=True)).astype(jnp.bfloat16)
        attended_blk = jnp.einsum(
            "hqk,kd->qhd", attn_weights, value_blk, preferred_element_type=jnp.float32
        )
        return attended_blk.astype(jnp.bfloat16)

    result = lax.map(
        one_block,
        (
            queries.reshape(blocks, SPAN, heads_here, HEAD_DIM),
            key_mine.reshape(blocks, SPAN, HEAD_DIM),
            value_mine.reshape(blocks, SPAN, HEAD_DIM),
            span_ids.reshape(blocks, SPAN),
        ),
    )
    return result.reshape(tokens_all, head_width)


def shards(
    queries, keys, values, span_ids, residual, norm_gain, routes, gates, w_gate, w_up, w_down
):
    devices = lax.axis_size("expert")
    tok_local = residual.shape[0]
    joined = jnp.concatenate(
        [
            keys.reshape(tok_local, KV_HEADS, HEAD_DIM),
            values.reshape(tok_local, KV_HEADS, HEAD_DIM),
        ],
        axis=2,
    )
    spread = jnp.repeat(joined, devices // KV_HEADS, axis=1)
    arrived_heads = lax.all_to_all(spread, "expert", split_axis=1, concat_axis=0, tiled=True)
    key_mine = arrived_heads[:, 0, :HEAD_DIM]
    value_mine = arrived_heads[:, 0, HEAD_DIM:]
    attended_heads = attend(queries, key_mine, value_mine, span_ids)
    attended = lax.all_to_all(attended_heads, "expert", split_axis=0, concat_axis=1, tiled=True)
    return experts(attended, residual, norm_gain, routes, gates, w_gate, w_up, w_down)


def solution(mesh):
    return jax.shard_map(
        shards,
        mesh=mesh,
        in_specs=(
            P("dp", "expert"),
            P(("dp", "expert"), None),
            P(("dp", "expert"), None),
            P("dp"),
            P(("dp", "expert"), None),
            P(),
            P(("dp", "expert"), None),
            P(("dp", "expert"), None),
            P("expert", None),
            P("expert", None),
            P("expert", None),
        ),
        out_specs=P(("dp", "expert"), None),
        check_vma=False,
    )
```

time: 172 us -> 87.7 us (0.51)
  waiting for transfers between devices: 107 us -> 20.3 us
  Pallas kernels: 0 us -> 42.9 us
  blocking collectives: 12.7 us -> 0 us
  matrix products: 14.6 us -> 4.09 us
  other arithmetic: 10.4 us -> 0.51 us
  starting transfers between devices: 15.3 us -> 10.6 us
  local copies, waits for them, and re-layouts: 11.8 us -> 8.53 us
    all_to_all x1 -> x0, waiting for transfers between devices: 48.4 us -> none  [shards(): lax.all_to_all(piece, 'expert', split_axis=0, concat_axis=0, tiled=True)]
    pallas_call x0 -> x1, Pallas kernels: none -> 42.9 us  [experts(): pl.pallas_call(functools.partial(moe_kernel, group), out_shape=jax.ShapeD...]
    ppermute x3 -> x0, waiting for transfers between devices: 39 us -> none  [from_partner(): return lax.ppermute(value, axis, pairs)]
    all_to_all x1 -> x0, blocking collectives: 12.7 us -> none  [shards(): lax.all_to_all(outgoing, 'expert', split_axis=0, concat_axis=0, tiled=True)]
    dot_general x3 -> x0, matrix products: 10.4 us -> none  [the longest x1 6.19 us: shards(): jnp.dot(hidden, w_down, preferred_element_type=jnp.float32)]
    gather x2 -> x0, local copies, waits for them, and re-layouts: 4.43 us -> none  [shards(): jnp.take(expert_out.reshape(wave * capacity, model_width), flat_slots.res...]
    select_n x3 -> x0, other arithmetic: 4.24 us -> none  [the longest x2 4.23 us: shards(): jnp.where(lower, jnp.concatenate([gathered, partner], axis=1), jnp.concat...]
    reduce_sum x4 -> x0, other arithmetic: 3.87 us -> none  [the longest x1 1.96 us: shards(): jnp.sum(returned.reshape(wave, group, capacity, model_width).astype(jnp.f...]
  transfers between devices with their start and end apart: 6 -> 2, of which waited for: 6 -> 2; matrix products, arithmetic and copies ran while one was open for 1% -> 1% of each run, Pallas kernels for 0% -> 0%
where the time goes in v2:
time: 87.7 us; the launch traced here: 87.2 us
  Pallas kernels  42.9 us (49%)
  waiting for transfers between devices  20.3 us (23%)
  starting transfers between devices  10.6 us (12%)
  local copies, waits for them, and re-layouts  8.53 us (10%)
  matrix products  4.09 us (5%)
    pallas_call x1, Pallas kernels, experts(): pl.pallas_call(functools.partial(moe_kernel, group), out_shape=jax.ShapeD...  42.9 us
    all_to_all x1, waiting for transfers between devices, shards(): lax.all_to_all(attended_heads, 'expert', split_axis=0, concat_axis=1, til...  10.4 us
    all_to_all x1, waiting for transfers between devices, shards(): lax.all_to_all(spread, 'expert', split_axis=1, concat_axis=0, tiled=True)  9.91 us
    all_to_all x1, starting transfers between devices, shards(): lax.all_to_all(spread, 'expert', split_axis=1, concat_axis=0, tiled=True)  7.3 us
    all_to_all x1, starting transfers between devices, shards(): lax.all_to_all(attended_heads, 'expert', split_axis=0, concat_axis=1, til...  3.32 us
    all_to_all x2, local copies, waits for them, and re-layouts, shards(): lax.all_to_all(attended_heads, 'expert', split_axis=0, concat_axis=1, til...  3.09 us
    dot_general x2, matrix products, one_block(): jnp.einsum('hqk,kd->qhd', attn_weights, value_blk, preferred_element_type...  2.26 us
    sub x2, matrix products, one_block(): raised = jnp.exp(scores - highest)  1.82 us
  transfers between devices with their start and end apart: 2, of which 2 were waited for; matrix products, arithmetic and copies ran while one was open for 1% of the time, Pallas kernels for 0%

profile of v2, /device:TPU:0, one launch (start us, length us, event | category | flops | bytes accessed | tf_op | source)
XLA Modules:
  0.0 87.2 jit_solution(1670308814724947996)
XLA Ops:
  0.0 0.0 copy-start.5
  0.0 0.8 reshape.59
  0.9 0.8 reshape.60
  1.7 0.1 pad_maximum_fusion
  1.8 0.7 broadcast_in_dim.30
  2.5 0.0 copy-start.8
  2.5 7.3 %all-to-all-start = ((bf16[32,32,128]{2,0,1:T(8,128)(2,1)}), bf16[32,32,128]{2,0,1:T(8,128)(2,1)S(1)}, u32[]{:S(2)}, u32[]{:S(2)}) async-start(bf16[32,32,128]{2,0,1:T(8,128)(2,1)} %bitcast), calls=%async_computation | async-start | bytes 524288 | tf_op jit(solution)/shard_map/all_to_all | solution.py:267
  9.8 0.0 copy-done.5
  9.8 0.2 reshape.67
  10.1 0.4 copy.22
  10.5 0.0 copy-done.8
  10.5 9.9 %all-to-all-done = bf16[32,32,128]{2,0,1:T(8,128)(2,1)S(1)} async-done(((bf16[32,32,128]{2,0,1:T(8,128)(2,1)}), bf16[32,32,128]{2,0,1:T(8,128)(2,1)S(1)}, u32[]{:S(2)}, u32[]{:S(2)}) %all-to-all-start) | async-done | bytes 262176 | tf_op jit(solution)/shard_map/all_to_all | solution.py:267
  20.4 0.1 fusion.54
  20.6 0.1 copy.20
  20.7 0.1 copy.21
  20.8 0.0 copy-start.2
  20.9 4.6 %while.11 = (s32[]{:T(128)}, bf16[2,512,2,64]{1,3,2,0:T(8,128)(2,1)S(1)}, bf16[2,512,64]{1,2,0:T(8,128)(2,1)S(1)}, s32[2,512]{1,0:T(2,128)S(1)}, bf16[2,512,64]{...) while((s32[]{:T(128)}, bf16[2,512,2,64]{1,3,2,0:T(8,128)(2,1)S(1)}, ...), condition=%wide.region_3.4_spmd.clone, body=%wide.region_0.3_spmd.clone.sunk | while | flops 206899200 | bytes 1393745 | solution.py:242
  20.9 0.2 fusion.69
  21.1 0.9 %fusion.70 = f32[2,512]{1,0:T(2,128)S(1)} fusion(pred[512,512]{0,1:T(8,128)(4,1)S(1)} %fusion.69, bf16[2,512,2,64]{1,3,2,0:T(8,128)(2,1)S(1)} %get-tuple-element.133, s32[]{:T(128)} %get-tuple-element.121, bf16[2,512,64]{1,2,0:T(8,128)(2,1)S(1)} %get-tuple-element.132), kind=kOutput, calls=%fused_computation.36.clone.1 | convolution fusion | flops 69206528 | bytes 463872 | tf_op jit(solution)/shard_map/while/body/eval_jaxpr/sub | solution.py:235
  22.0 1.1 %fusion.71 = bf16[2,512,2,64]{1,3,2,0:T(8,128)(2,1)S(1)} fusion(bf16[2,512,2,64]{1,3,2,0:T(8,128)(2,1)S(1)} %get-tuple-element.122, s32[]{:T(128)} %get-tuple-element.121, f32[2,512]{1,0:T(2,128)S(1)} %fusion.70, bf16[2,512,64]{1,2,0:T(8,128)(2,1)S(1)} %get-tuple-element.130, pred[512,512]{0,1:T(8,128)(4,1)S(1)} %fusion.69, ...), kind=kOutput, calls=%fused_computation.8.clone.1 | convolution fusion | flops 136906240 | bytes 661504 | tf_op jit(solution)/shard_map/while/body/eval_jaxpr/hqk,kd->qhd/dot_general | solution.py:237
  23.2 0.2 fusion.69
  23.4 0.9 %fusion.70 = f32[2,512]{1,0:T(2,128)S(1)} fusion(pred[512,512]{0,1:T(8,128)(4,1)S(1)} %fusion.69, bf16[2,512,2,64]{1,3,2,0:T(8,128)(2,1)S(1)} %get-tuple-element.133, s32[]{:T(128)} %get-tuple-element.121, bf16[2,512,64]{1,2,0:T(8,128)(2,1)S(1)} %get-tuple-element.132), kind=kOutput, calls=%fused_computation.36.clone.1 | convolution fusion | flops 69206528 | bytes 463872 | tf_op jit(solution)/shard_map/while/body/eval_jaxpr/sub | solution.py:235
  24.3 1.1 %fusion.71 = bf16[2,512,2,64]{1,3,2,0:T(8,128)(2,1)S(1)} fusion(bf16[2,512,2,64]{1,3,2,0:T(8,128)(2,1)S(1)} %get-tuple-element.122, s32[]{:T(128)} %get-tuple-element.121, f32[2,512]{1,0:T(2,128)S(1)} %fusion.70, bf16[2,512,64]{1,2,0:T(8,128)(2,1)S(1)} %get-tuple-element.130, pred[512,512]{0,1:T(8,128)(4,1)S(1)} %fusion.69, ...), kind=kOutput, calls=%fused_computation.8.clone.1 | convolution fusion | flops 136906240 | bytes 661504 | tf_op jit(solution)/shard_map/while/body/eval_jaxpr/hqk,kd->qhd/dot_general | solution.py:237
  25.5 0.0 copy-start.6
  25.5 0.0 copy-start.7
  25.5 0.0 copy-start.1
  25.5 1.1 %copy.23 = bf16[2,512,2,64]{3,2,1,0:T(2,128)(2,1)} copy(bf16[2,512,2,64]{1,3,2,0:T(8,128)(2,1)S(1)} %get-tuple-element.42) | data formatting | bytes 524288 | tf_op jit(solution)/shard_map/while | solution.py:242
  26.6 0.0 copy-start
  26.6 0.0 copy-start.3
  26.6 0.0 copy-start.4
  26.6 2.1 %all_to_all.31 = bf16[32,32,128]{2,1,0:T(8,128)(2,1)} reshape(bf16[2,512,2,64]{3,2,1,0:T(2,128)(2,1)} %copy.23) | data formatting | bytes 524288 | tf_op jit(solution)/shard_map/all_to_all | solution.py:271
  28.7 3.3 %all-to-all-start.1 = ((bf16[32,32,128]{2,1,0:T(8,128)(2,1)}), bf16[32,32,128]{2,1,0:T(8,128)(2,1)}, u32[]{:S(2)}, u32[]{:S(2)}) async-start(bf16[32,32,128]{2,1,0:T(8,128)(2,1)} %all_to_all.31), calls=%async_computation.1 | async-start | bytes 524288 | tf_op jit(solution)/shard_map/all_to_all | solution.py:271
  32.0 0.0 copy-done.6
  32.0 0.1 copy.25.routes
  32.1 0.0 copy-done.7
  32.1 0.1 copy.26.gates
  32.2 10.4 %all-to-all-done.1 = bf16[32,32,128]{2,1,0:T(8,128)(2,1)} async-done(((bf16[32,32,128]{2,1,0:T(8,128)(2,1)}), bf16[32,32,128]{2,1,0:T(8,128)(2,1)}, u32[]{:S(2)}, u32[]{:S(2)}) %all-to-all-start.1) | async-done | bytes 262176 | tf_op jit(solution)/shard_map/all_to_all | solution.py:271
  42.6 1.0 %copy_bitcast_fusion.att = bf16[32,4096]{1,0:T(8,128)(2,1)S(1)} fusion(bf16[32,32,128]{2,1,0:T(8,128)(2,1)} %all-to-all-done.1), kind=kLoop, calls=%fused_computation.34 | loop fusion | bytes 524288 | tf_op jit(solution)/shard_map/all_to_all | solution.py:271
  43.6 0.0 copy-done.2
  43.6 0.0 copy-done.1
  43.6 0.0 copy-done
  43.6 0.0 copy-done.3
  43.6 0.0 copy-done.4
  43.6 42.9 %shard_map.109 = bf16[32,4096]{1,0:T(8,128)(2,1)S(1)} custom-call(bf16[32,4096]{1,0:T(8,128)(2,1)S(1)} %copy_bitcast_fusion.att, bf16[32,4096]{1,0:T(8,128)(2,1)S(1)} %copy-done.3, f32[1,4096]{1,0:T(1,128)S(1)} %bitcast.82, s32[32,8]{1,0:T(8,128)S(1)} %copy.25.routes, f32[32,8]{1,0:T(8,128)S(1)} %copy.26.gates, bf16[128,4096]{1,0:T(8,128)(2,1)S(1)} %copy-done, ...), custom_call_target="tpu_custom_call" | custom-call | tf_op jit(solution)/shard_map/pallas_call | solution.py:193
  86.5 0.7 copy.46
  (5 shorter events, 0.0 us)
Async XLA Ops:
  0.0 9.8 %copy-start.5 = (bf16[1024,128]{1,0:T(8,128)(2,1)S(1)}, bf16[1024,128]{1,0:T(8,128)(2,1)}, u32[]{:S(2)}) copy-start(bf16[1024,128]{1,0:T(8,128)(2,1)} %param.13) | copy-start | bytes 786436
  2.5 8.0 %copy-start.8 = (s32[1024]{0:T(1024)S(1)}, s32[1024]{0:T(1024)}, u32[]{:S(2)}) copy-start(s32[1024]{0:T(1024)} %param.16) | copy-start | bytes 12292
  2.5 17.9 %all-to-all-start = ((bf16[32,32,128]{2,0,1:T(8,128)(2,1)}), bf16[32,32,128]{2,0,1:T(8,128)(2,1)S(1)}, u32[]{:S(2)}, u32[]{:S(2)}) async-start(bf16[32,32,128]{2,0,1:T(8,128)(2,1)} %bitcast), calls=%async_computation | async-start | bytes 524288 | tf_op jit(solution)/shard_map/all_to_all | solution.py:267
  20.8 22.7 %copy-start.2 = (bf16[128,4096]{1,0:T(8,128)(2,1)S(1)}, bf16[128,4096]{1,0:T(8,128)(2,1)}, u32[]{:S(2)}) copy-start(bf16[128,4096]{1,0:T(8,128)(2,1)} %wd.1) | copy-start | bytes 3145732
  25.5 6.6 %copy-start.6 = (s32[32,8]{0,1:T(8,128)S(1)}, s32[32,8]{0,1:T(8,128)}, u32[]{:S(2)}) copy-start(s32[32,8]{0,1:T(8,128)} %param.19) | copy-start | bytes 3076
  25.5 6.7 %copy-start.7 = (f32[32,8]{0,1:T(8,128)S(1)}, f32[32,8]{0,1:T(8,128)}, u32[]{:S(2)}) copy-start(f32[32,8]{0,1:T(8,128)} %param.20) | copy-start | bytes 3076
  25.5 18.1 %copy-start.1 = (bf16[128,4096]{1,0:T(8,128)(2,1)S(1)}, bf16[128,4096]{1,0:T(8,128)(2,1)}, u32[]{:S(2)}) copy-start(bf16[128,4096]{1,0:T(8,128)(2,1)} %wu.1) | copy-start | bytes 3145732
  26.6 17.0 %copy-start = (bf16[128,4096]{1,0:T(8,128)(2,1)S(1)}, bf16[128,4096]{1,0:T(8,128)(2,1)}, u32[]{:S(2)}) copy-start(bf16[128,4096]{1,0:T(8,128)(2,1)} %wg.1) | copy-start | bytes 3145732
  26.6 17.0 %copy-start.3 = (bf16[32,4096]{1,0:T(8,128)(2,1)S(1)}, bf16[32,4096]{1,0:T(8,128)(2,1)}, u32[]{:S(2)}) copy-start(bf16[32,4096]{1,0:T(8,128)(2,1)} %res.1) | copy-start | bytes 786436
  26.6 17.0 %copy-start.4 = (f32[4096]{0:T(1024)S(1)}, f32[4096]{0:T(1024)}, u32[]{:S(2)}) copy-start(f32[4096]{0:T(1024)} %param.18) | copy-start | bytes 49156
  28.7 13.9 %all-to-all-start.1 = ((bf16[32,32,128]{2,1,0:T(8,128)(2,1)}), bf16[32,32,128]{2,1,0:T(8,128)(2,1)}, u32[]{:S(2)}, u32[]{:S(2)}) async-start(bf16[32,32,128]{2,1,0:T(8,128)(2,1)} %all_to_all.31), calls=%async_computation.1 | async-start | bytes 524288 | tf_op jit(solution)/shard_map/all_to_all | solution.py:271

commit v3 on v2

--- a/solution.py
+++ b/solution.py
@@ -48,7 +48,9 @@
 
 
 def moe_kernel(
-    group, att, res, gain, routes, gates, wg, wu, wd, out,
+    group, queries, keys, values, ids, res, gain, routes, gates, wg, wu, wd, out,
+    kv_out, kv_buf, id_rows, att_in, att_own, att_buf,
+    kz_send, kv_send, kv_recv, az_send, az_recv, a_send, a_recv,
     wgu_v, wd_v, outg, x_buf, part, core_buf, sums, plane_buf, final, back,
     w_sem, z_send, x_send, x_recv, c_send, c_recv, p_send, p_recv, b_send, b_recv,
 ):
@@ -76,30 +78,99 @@
     for copy in weights:
         copy.start()
     barrier = pltpu.get_barrier_semaphore()
-    partners = [across(rz) for rz in range(1, wave)] + [within(r) for r in (1, 2, 4, 6)]
+    partners = [across(rz) for rz in range(1, wave)] + [within(r) for r in range(1, group)]
     for device in partners:
         pl.semaphore_signal(barrier, inc=1, device_id={"expert": device}, device_id_type=MESH)
 
+    for plane_to in range(wave):
+        head = plane_to * KV_HEADS // wave
+        columns = slice(head * HEAD_DIM, (head + 1) * HEAD_DIM)
+        kv_out[plane_to] = jnp.concatenate([keys[:, columns], values[:, columns]], axis=1)
+    pl.semaphore_wait(barrier, len(partners))
+
+    sends = []
+
+    def go(copy):
+        copy.start()
+        sends.append(copy)
+        return copy
+
+    def arrived(ref, sem):
+        pltpu.make_async_copy(ref, ref, sem).wait()
+
+    for rz in range(1, wave):
+        go(remote(kv_out.at[plane ^ rz], kv_buf.at[plane, mine], kz_send.at[rz], kv_recv.at[rz, 0], across(rz)))
+    kv_buf[plane, mine] = kv_out[plane]
+    for rz in range(wave):
+        block = kv_buf.at[plane ^ rz, mine]
+        if rz:
+            arrived(block, kv_recv.at[rz, 0])
+        for r in range(1, group):
+            go(remote(block, block, kv_send.at[rz, r], kv_recv.at[rz, r], within(r)))
+
     chosen, mix = route_matrix(routes[...], gates[...], wave, capacity)
-    stream = (res[...].astype(F32) + att[...].astype(F32)).astype(BF16).astype(F32)
+    chunk = group * tokens
+    for index in range(wave):
+        id_rows[index] = jnp.broadcast_to(ids[index].astype(F32), (128, chunk)).T
+    for rz in range(wave):
+        for r in range(1, group):
+            arrived(kv_buf.at[plane ^ rz, mine ^ r], kv_recv.at[rz, r])
+
+    def attend(index):
+        planes = SPAN // chunk
+        first = index // planes * planes
+        block = kv_buf[pl.ds(first, planes)].reshape(SPAN, 2 * HEAD_DIM)
+        key_blk = block[:, :HEAD_DIM]
+        value_rows = block.T[HEAD_DIM:]
+        key_ids = id_rows[pl.ds(first, planes)].reshape(SPAN, 128)
+        key_ids = jnp.concatenate([key_ids] * (chunk // 128), axis=1)
+        offset = (index - first) * chunk
+        ahead = (
+            lax.broadcasted_iota(jnp.int32, (SPAN, chunk), 0)
+            - lax.broadcasted_iota(jnp.int32, (SPAN, chunk), 1)
+        )
+        allowed = (ahead <= offset) & (key_ids == ids[index].astype(F32))
+        query = queries[pl.ds(pl.multiple_of(index * chunk, chunk), chunk), :] * BF16(1.0 / math.sqrt(HEAD_DIM))
+        heads = []
+        for head in range(query.shape[1] // HEAD_DIM):
+            one = query[:, head * HEAD_DIM:(head + 1) * HEAD_DIM]
+            scores = lax.dot_general(key_blk, one, (((1,), (1,)), ((), ())), preferred_element_type=F32)
+            scores = jnp.where(allowed, scores, -jnp.inf)
+            raised = jnp.exp(scores - jnp.max(scores, axis=0, keepdims=True))
+            weights_here = raised * (1.0 / jnp.sum(raised, axis=0, keepdims=True))
+            heads.append(jnp.dot(value_rows, weights_here.astype(BF16), preferred_element_type=F32))
+        joined = heads[0] if len(heads) == 1 else jnp.concatenate(heads, axis=0)
+        return joined.T.astype(BF16).reshape(group, tokens, query.shape[1])
+
+    def spread(rz):
+        if rz:
+            arrived(att_in.at[rz], az_recv.at[rz])
+        target = att_buf.at[plane ^ rz, mine]
+        for r in range(1, group):
+            go(remote(att_in.at[rz, mine ^ r], target, a_send.at[rz, r], a_recv.at[rz, r], within(r)))
+        att_buf[plane ^ rz, mine] = att_in[rz, mine]
+
+    for rz in range(wave - 1, 0, -1):
+        att_own[rz] = attend(plane ^ rz)
+        go(remote(att_own.at[rz], att_in.at[rz], az_send.at[rz], az_recv.at[rz], across(rz)))
+        if rz < wave - 2:
+            spread(rz + 2)
+    att_in[0] = attend(plane)
+    for rz in range(min(2, wave - 1), -1, -1):
+        spread(rz)
+    for rz in range(wave):
+        for r in range(1, group):
+            arrived(att_buf.at[plane ^ rz, mine ^ r], a_recv.at[rz, r])
+    att = jnp.concatenate(
+        [att_buf[index // group, index % group] for index in range(wave * group)], axis=1
+    )
+    stream = (res[...].astype(F32) + att.astype(F32)).astype(BF16).astype(F32)
     inverse = lax.rsqrt(jnp.mean(stream * stream, axis=-1, keepdims=True) + 1e-06)
     normed = (stream * inverse * gain[...]).astype(BF16)
     rows = jnp.dot(chosen.T.astype(BF16), normed, preferred_element_type=F32)
     for expert in range(wave):
         block = rows[expert * capacity:(expert + 1) * capacity]
         outg[expert] = jnp.concatenate([block[:, :half], block[:, half:]], axis=0).astype(BF16)
-    pl.semaphore_wait(barrier, len(partners))
-
-    sends = []
-
-    def go(copy):
-        copy.start()
-        sends.append(copy)
-        return copy
-
-    def arrived(ref, sem):
-        pltpu.make_async_copy(ref, ref, sem).wait()
-
     for rz in range(1, wave):
         go(remote(outg.at[plane ^ rz], x_buf.at[0, rz], z_send.at[rz], x_recv.at[0, rz], across(rz)))
     x_buf[0, 0] = outg[plane]
@@ -178,7 +249,7 @@
         copy.wait_send()
 
 
-def experts(att, res, gain, routes, gates, wg, wu, wd):
+def layer(queries, keys, values, span_ids, res, gain, routes, gates, wg, wu, wd):
     devices = lax.axis_size("expert")
     group = FF_WIN // wg.shape[0]
     wave = devices // group
@@ -193,9 +264,17 @@
     return pl.pallas_call(
         functools.partial(moe_kernel, group),
         out_shape=jax.ShapeDtypeStruct((tokens, width), BF16),
-        in_specs=[vmem] * 5 + [hbm] * 3,
+        in_specs=[vmem] * 8 + [hbm] * 3,
         out_specs=vmem,
         scratch_shapes=[
+            pltpu.VMEM((wave, tokens, 2 * HEAD_DIM), BF16),
+            pltpu.VMEM((wave, group, tokens, 2 * HEAD_DIM), BF16),
+            pltpu.VMEM((wave, group * tokens, 128), F32),
+            pltpu.VMEM((wave, group, tokens, queries.shape[1]), BF16),
+            pltpu.VMEM((wave, group, tokens, queries.shape[1]), BF16),
+            pltpu.VMEM((wave, group, tokens, queries.shape[1]), BF16),
+            dma((wave,)), dma((wave, group)), dma((wave, group)),
+            dma((wave,)), dma((wave,)), dma((wave, group)), dma((wave, group)),
             pltpu.VMEM((2 * wg.shape[0], width), BF16),
             pltpu.VMEM((wd.shape[0], width), BF16),
             pltpu.VMEM((wave, 2 * capacity, half), BF16),
@@ -212,69 +291,12 @@
         compiler_params=pltpu.CompilerParams(
             collective_id=0, has_side_effects=True, vmem_limit_bytes=48 * 2**20
         ),
-    )(att, res, gain.reshape(1, width), routes, gates, wg, wu, wd)
-
-
-def attend(queries, key_mine, value_mine, span_ids):
-    tokens_all, head_width = queries.shape
-    heads_here = head_width // HEAD_DIM
-    blocks = tokens_all // SPAN
-    score_scale = 1.0 / math.sqrt(HEAD_DIM)
-    positions = jnp.arange(SPAN)
-    causal = positions[None, :] <= positions[:, None]
-
-    def one_block(pieces):
-        query_blk, key_blk, value_blk, ids_blk = pieces
-        scores = (
-            jnp.einsum("qhd,kd->hqk", query_blk, key_blk, preferred_element_type=jnp.float32)
-            * score_scale
-        )
-        allowed = causal & (ids_blk[None, :] == ids_blk[:, None])
-        scores = jnp.where(allowed[None], scores, -jnp.inf)
-        highest = jnp.max(scores, axis=-1, keepdims=True)
-        raised = jnp.exp(scores - highest)
-        attn_weights = (raised / jnp.sum(raised, axis=-1, keepdims=True)).astype(jnp.bfloat16)
-        attended_blk = jnp.einsum(
-            "hqk,kd->qhd", attn_weights, value_blk, preferred_element_type=jnp.float32
-        )
-        return attended_blk.astype(jnp.bfloat16)
-
-    result = lax.map(
-        one_block,
-        (
-            queries.reshape(blocks, SPAN, heads_here, HEAD_DIM),
-            key_mine.reshape(blocks, SPAN, HEAD_DIM),
-            value_mine.reshape(blocks, SPAN, HEAD_DIM),
-            span_ids.reshape(blocks, SPAN),
-        ),
-    )
-    return result.reshape(tokens_all, head_width)
-
-
-def shards(
-    queries, keys, values, span_ids, residual, norm_gain, routes, gates, w_gate, w_up, w_down
-):
-    devices = lax.axis_size("expert")
-    tok_local = residual.shape[0]
-    joined = jnp.concatenate(
-        [
-            keys.reshape(tok_local, KV_HEADS, HEAD_DIM),
-            values.reshape(tok_local, KV_HEADS, HEAD_DIM),
-        ],
-        axis=2,
-    )
-    spread = jnp.repeat(joined, devices // KV_HEADS, axis=1)
-    arrived_heads = lax.all_to_all(spread, "expert", split_axis=1, concat_axis=0, tiled=True)
-    key_mine = arrived_heads[:, 0, :HEAD_DIM]
-    value_mine = arrived_heads[:, 0, HEAD_DIM:]
-    attended_heads = attend(queries, key_mine, value_mine, span_ids)
-    attended = lax.all_to_all(attended_heads, "expert", split_axis=0, concat_axis=1, tiled=True)
-    return experts(attended, residual, norm_gain, routes, gates, w_gate, w_up, w_down)
+    )(queries, keys, values, span_ids.reshape(wave, 1, group * tokens), res, gain.reshape(1, width), routes, gates, wg, wu, wd)
 
 
 def solution(mesh):
     return jax.shard_map(
-        shards,
+        layer,
         mesh=mesh,
         in_specs=(
             P("dp", "expert"),

time: 87.7 us -> 78.5 us (0.90)
  Pallas kernels: 42.9 us -> 69.6 us
  waiting for transfers between devices: 20.3 us -> 0 us
  starting transfers between devices: 10.6 us -> 0 us
  matrix products: 4.09 us -> 0 us
    pallas_call x1, Pallas kernels: 42.9 us -> 69.6 us  [layer(): pl.pallas_call(functools.partial(moe_kernel, group), out_shape=jax.ShapeD...]
    all_to_all x2 -> x0, waiting for transfers between devices: 20.3 us -> none  [the longest x1 10.4 us: shards(): lax.all_to_all(attended_heads, 'expert', split_axis=0, concat_axis=1, til...]
    all_to_all x2 -> x0, starting transfers between devices: 10.6 us -> none  [the longest x1 7.3 us: shards(): lax.all_to_all(spread, 'expert', split_axis=1, concat_axis=0, tiled=True)]
    unnamed x24 -> x23, local copies, waits for them, and re-layouts: 1.54 us -> 8.48 us
    all_to_all x2 -> x0, local copies, waits for them, and re-layouts: 3.09 us -> none  [shards(): lax.all_to_all(attended_heads, 'expert', split_axis=0, concat_axis=1, til...]
    dot_general x2 -> x0, matrix products: 2.26 us -> none  [one_block(): jnp.einsum('hqk,kd->qhd', attn_weights, value_blk, preferred_element_type...]
    reshape x4 -> x0, local copies, waits for them, and re-layouts: 1.91 us -> none  [the longest x1 0.85 us: shards(): keys.reshape(tok_local, KV_HEADS, HEAD_DIM)]
    sub x2 -> x0, matrix products: 1.82 us -> none  [one_block(): raised = jnp.exp(scores - highest)]
  transfers between devices with their start and end apart: 2 -> 0, of which waited for: 2 -> 0; matrix products, arithmetic and copies ran while one was open for 1% -> 0% of each run, Pallas kernels for 0% -> 0%
where the time goes in v3:
time: 78.5 us; the launch traced here: 78.1 us
  Pallas kernels  69.6 us (89%)
  local copies, waits for them, and re-layouts  8.48 us (11%)
    pallas_call x1, Pallas kernels, layer(): pl.pallas_call(functools.partial(moe_kernel, group), out_shape=jax.ShapeD...  69.6 us
    unnamed x23, local copies, waits for them, and re-layouts  8.48 us

profile of v3, /device:TPU:0, one launch (start us, length us, event | category | flops | bytes accessed | tf_op | source)
XLA Modules:
  0.0 78.1 jit_solution(3753092258676858328)
XLA Ops:
  0.0 0.0 copy-start.9
  0.0 0.0 copy-start.5
  0.0 0.0 copy-start.6
  0.0 0.8 %copy.12.routes = s32[32,8]{1,0:T(8,128)S(1)} copy(s32[32,8]{0,1:T(8,128)} %param.17) | data formatting | bytes 2048 | tf_op args[6]
  0.8 0.0 copy-done.9
  0.8 0.0 copy-start.8
  0.8 0.1 copy.13.gates
  0.9 0.0 copy-done.5
  0.9 0.0 copy-done.6
  0.9 0.6 copy-done.8
  1.5 0.0 copy-start
  1.5 1.2 %copy-done = bf16[128,4096]{1,0:T(8,128)(2,1)S(1)} copy-done((bf16[128,4096]{1,0:T(8,128)(2,1)S(1)}, bf16[128,4096]{1,0:T(8,128)(2,1)}, u32[]{:S(2)}) %copy-start) | copy-done | bytes 1048600
  2.7 0.0 copy-start.1
  2.7 1.2 %copy-done.1 = bf16[128,4096]{1,0:T(8,128)(2,1)S(1)} copy-done((bf16[128,4096]{1,0:T(8,128)(2,1)S(1)}, bf16[128,4096]{1,0:T(8,128)(2,1)}, u32[]{:S(2)}) %copy-start.1) | copy-done | bytes 1048600
  3.9 0.0 copy-start.2
  3.9 1.2 %copy-done.2 = bf16[128,4096]{1,0:T(8,128)(2,1)S(1)} copy-done((bf16[128,4096]{1,0:T(8,128)(2,1)S(1)}, bf16[128,4096]{1,0:T(8,128)(2,1)}, u32[]{:S(2)}) %copy-start.2) | copy-done | bytes 1048600
  5.2 0.0 copy-start.3
  5.2 0.9 %copy-done.3 = bf16[1024,128]{1,0:T(8,128)(2,1)S(1)} copy-done((bf16[1024,128]{1,0:T(8,128)(2,1)S(1)}, bf16[1024,128]{1,0:T(8,128)(2,1)}, u32[]{:S(2)}) %copy-start.3) | copy-done | bytes 262168
  6.1 0.0 copy-start.4
  6.1 0.9 %copy-done.4 = bf16[32,4096]{1,0:T(8,128)(2,1)S(1)} copy-done((bf16[32,4096]{1,0:T(8,128)(2,1)S(1)}, bf16[32,4096]{1,0:T(8,128)(2,1)}, u32[]{:S(2)}) %copy-start.4) | copy-done | bytes 262168
  7.1 0.0 copy-start.7
  7.1 0.7 copy-done.7
  7.8 69.6 %shard_map.109 = bf16[32,4096]{1,0:T(8,128)(2,1)S(1)} custom-call(bf16[1024,128]{1,0:T(8,128)(2,1)S(1)} %copy-done.3, bf16[32,256]{1,0:T(8,128)(2,1)S(1)} %copy-done.5, bf16[32,256]{1,0:T(8,128)(2,1)S(1)} %copy-done.6, s32[4,1,256]{2,1,0:T(1,128)S(1)} %bitcast.3, bf16[32,4096]{1,0:T(8,128)(2,1)S(1)} %copy-done.4, f32[1,4096]{1,0:T(1,128)S(1)} %bitcast.2, ...), custom_call_target="tpu_custom_call" | custom-call | tf_op jit(solution)/shard_map/pallas_call | solution.py:264
  77.4 0.7 copy.15
Async XLA Ops:
  0.0 0.8 %copy-start.9 = (f32[32,8]{0,1:T(8,128)S(1)}, f32[32,8]{0,1:T(8,128)}, u32[]{:S(2)}) copy-start(f32[32,8]{0,1:T(8,128)} %param.18) | copy-start | bytes 3076
  0.0 0.9 %copy-start.5 = (bf16[32,256]{1,0:T(8,128)(2,1)S(1)}, bf16[32,256]{1,0:T(8,128)(2,1)}, u32[]{:S(2)}) copy-start(bf16[32,256]{1,0:T(8,128)(2,1)} %keys.1) | copy-start | bytes 49156
  0.0 0.9 %copy-start.6 = (bf16[32,256]{1,0:T(8,128)(2,1)S(1)}, bf16[32,256]{1,0:T(8,128)(2,1)}, u32[]{:S(2)}) copy-start(bf16[32,256]{1,0:T(8,128)(2,1)} %values.1) | copy-start | bytes 49156
  0.8 0.7 copy-start.8
  1.5 1.2 %copy-start = (bf16[128,4096]{1,0:T(8,128)(2,1)S(1)}, bf16[128,4096]{1,0:T(8,128)(2,1)}, u32[]{:S(2)}) copy-start(bf16[128,4096]{1,0:T(8,128)(2,1)} %wg.1) | copy-start | bytes 3145732
  2.7 1.2 %copy-start.1 = (bf16[128,4096]{1,0:T(8,128)(2,1)S(1)}, bf16[128,4096]{1,0:T(8,128)(2,1)}, u32[]{:S(2)}) copy-start(bf16[128,4096]{1,0:T(8,128)(2,1)} %wu.1) | copy-start | bytes 3145732
  3.9 1.2 %copy-start.2 = (bf16[128,4096]{1,0:T(8,128)(2,1)S(1)}, bf16[128,4096]{1,0:T(8,128)(2,1)}, u32[]{:S(2)}) copy-start(bf16[128,4096]{1,0:T(8,128)(2,1)} %wd.1) | copy-start | bytes 3145732
  5.2 0.9 %copy-start.3 = (bf16[1024,128]{1,0:T(8,128)(2,1)S(1)}, bf16[1024,128]{1,0:T(8,128)(2,1)}, u32[]{:S(2)}) copy-start(bf16[1024,128]{1,0:T(8,128)(2,1)} %queries.1) | copy-start | bytes 786436
  6.1 0.9 %copy-start.4 = (bf16[32,4096]{1,0:T(8,128)(2,1)S(1)}, bf16[32,4096]{1,0:T(8,128)(2,1)}, u32[]{:S(2)}) copy-start(bf16[32,4096]{1,0:T(8,128)(2,1)} %res.1) | copy-start | bytes 786436
  7.1 0.7 copy-start.7

commit v4 on v3

--- a/solution.py
+++ b/solution.py
@@ -48,7 +48,8 @@
 
 
 def moe_kernel(
-    group, queries, keys, values, ids, res, gain, routes, gates, wg, wu, wd, out,
+    group, queries_hbm, keys_hbm, values_hbm, ids_hbm, res_hbm, gain_hbm, routes_hbm, gates_hbm, wg, wu, wd, out,
+    queries, keys, values, ids, res, gain, routes, gates, in_sem,
     kv_out, kv_buf, id_rows, att_in, att_own, att_buf,
     kz_send, kv_send, kv_recv, az_send, az_recv, a_send, a_recv,
     wgu_v, wd_v, outg, x_buf, part, core_buf, sums, plane_buf, final, back,
@@ -57,7 +58,7 @@
     me = lax.axis_index("expert")
     wave = outg.shape[0]
     capacity = outg.shape[1] // 2
-    tokens, width = res.shape
+    tokens, width = out.shape
     half = width // 2
     hidden_here = wg.shape[0]
     mine = me % group
@@ -70,18 +71,27 @@
     def within(r):
         return base + (mine ^ r)
 
+    fetched = {}
+    for number, (name, source, target) in enumerate((
+        ("keys", keys_hbm, keys), ("values", values_hbm, values), ("ids", ids_hbm, ids),
+        ("routes", routes_hbm, routes), ("gates", gates_hbm, gates), ("queries", queries_hbm, queries),
+        ("res", res_hbm, res), ("gain", gain_hbm, gain),
+    )):
+        fetched[name] = pltpu.make_async_copy(source, target, in_sem.at[number])
     weights = [
         pltpu.make_async_copy(wg, wgu_v.at[pl.ds(0, hidden_here)], w_sem.at[0]),
         pltpu.make_async_copy(wu, wgu_v.at[pl.ds(hidden_here, hidden_here)], w_sem.at[1]),
         pltpu.make_async_copy(wd, wd_v, w_sem.at[2]),
     ]
-    for copy in weights:
-        copy.start()
     barrier = pltpu.get_barrier_semaphore()
     partners = [across(rz) for rz in range(1, wave)] + [within(r) for r in range(1, group)]
     for device in partners:
         pl.semaphore_signal(barrier, inc=1, device_id={"expert": device}, device_id_type=MESH)
 
+    for copy in list(fetched.values()) + weights:
+        copy.start()
+    for name in ("keys", "values"):
+        fetched[name].wait()
     for plane_to in range(wave):
         head = plane_to * KV_HEADS // wave
         columns = slice(head * HEAD_DIM, (head + 1) * HEAD_DIM)
@@ -105,16 +115,18 @@
         block = kv_buf.at[plane ^ rz, mine]
         if rz:
             arrived(block, kv_recv.at[rz, 0])
-        for r in range(1, group):
-            go(remote(block, block, kv_send.at[rz, r], kv_recv.at[rz, r], within(r)))
-
-    chosen, mix = route_matrix(routes[...], gates[...], wave, capacity)
+    for r in range(1, group):
+        block = kv_buf.at[:, mine]
+        go(remote(block, block, kv_send.at[0, r], kv_recv.at[0, r], within(r)))
+
+    for name in ("ids", "routes", "gates", "queries"):
+        fetched[name].wait()
+    chosen, mix = route_matrix(routes[...].astype(F32).T, gates[...].T, wave, capacity)
     chunk = group * tokens
     for index in range(wave):
         id_rows[index] = jnp.broadcast_to(ids[index].astype(F32), (128, chunk)).T
-    for rz in range(wave):
-        for r in range(1, group):
-            arrived(kv_buf.at[plane ^ rz, mine ^ r], kv_recv.at[rz, r])
+    for r in range(1, group):
+        arrived(kv_buf.at[:, mine ^ r], kv_recv.at[0, r])
 
     def attend(index):
         planes = SPAN // chunk
@@ -164,6 +176,8 @@
     att = jnp.concatenate(
         [att_buf[index // group, index % group] for index in range(wave * group)], axis=1
     )
+    for name in ("res", "gain"):
+        fetched[name].wait()
     stream = (res[...].astype(F32) + att.astype(F32)).astype(BF16).astype(F32)
     inverse = lax.rsqrt(jnp.mean(stream * stream, axis=-1, keepdims=True) + 1e-06)
     normed = (stream * inverse * gain[...]).astype(BF16)
@@ -177,7 +191,7 @@
     for rz in range(wave):
         if rz:
             arrived(x_buf.at[0, rz], x_recv.at[0, rz])
-        for r in (2, 4, 6, 1):
+        for r in (2, 4, 1):
             go(remote(x_buf.at[0, rz], x_buf.at[r, rz], x_send.at[r, rz], x_recv.at[r, rz], within(r)))
     for copy in weights:
         copy.wait()
@@ -189,15 +203,24 @@
         if k:
             go(remote(sums.at[k], plane_buf.at[k], p_send.at[k], p_recv.at[k], within(2 * k)))
 
+    def landed(r, rz):
+        arrived(x_buf.at[r, rz], x_recv.at[r, rz])
+        go(remote(x_buf.at[r, rz], x_buf.at[r + 1, rz], x_send.at[r + 1, rz], x_recv.at[r + 1, rz], within(1)))
+
     dims = (((1,), (1,)), ((), ()))
     pairs = group // 2
     for k in range(pairs):
         r = 2 * k
-        if k:
+        if k == 1:
             for rz in range(wave):
-                arrived(x_buf.at[r, rz], x_recv.at[r, rz])
-                go(remote(x_buf.at[r, rz], x_buf.at[r + 1, rz], x_send.at[r + 1, rz],
-                          x_recv.at[r + 1, rz], within(1)))
+                for near, other in ((2, 4), (4, 2)):
+                    landed(near, rz)
+                    if (rz < wave // 2) == (near == 4):
+                        go(remote(x_buf.at[near, rz], x_buf.at[6, rz], x_send.at[6, rz],
+                                  x_recv.at[6, rz], within(other)))
+        if k == 3:
+            for rz in range(wave):
+                landed(6, rz)
         for rz in range(wave):
             arrived(x_buf.at[r + 1, rz], x_recv.at[r + 1, rz])
         x = x_buf[r:r + 2].reshape(2 * wave * 2 * capacity, half)
@@ -264,9 +287,18 @@
     return pl.pallas_call(
         functools.partial(moe_kernel, group),
         out_shape=jax.ShapeDtypeStruct((tokens, width), BF16),
-        in_specs=[vmem] * 8 + [hbm] * 3,
+        in_specs=[hbm] * 11,
         out_specs=vmem,
         scratch_shapes=[
+            pltpu.VMEM(queries.shape, BF16),
+            pltpu.VMEM(keys.shape, BF16),
+            pltpu.VMEM(values.shape, BF16),
+            pltpu.VMEM((wave, 1, group * tokens), jnp.int32),
+            pltpu.VMEM(res.shape, BF16),
+            pltpu.VMEM((1, width), F32),
+            pltpu.VMEM(routes.shape[::-1], jnp.int32),
+            pltpu.VMEM(gates.shape[::-1], F32),
+            dma((8,)),
             pltpu.VMEM((wave, tokens, 2 * HEAD_DIM), BF16),
             pltpu.VMEM((wave, group, tokens, 2 * HEAD_DIM), BF16),
             pltpu.VMEM((wave, group * tokens, 128), F32),
@@ -289,9 +321,9 @@
             dma((pairs,)), dma((pairs,)), dma((pairs,)), dma((pairs,)), dma((wave,)), dma((wave,)),
         ],
         compiler_params=pltpu.CompilerParams(
-            collective_id=0, has_side_effects=True, vmem_limit_bytes=48 * 2**20
+            collective_id=0, has_side_effects=True, vmem_limit_bytes=60 * 2**20
         ),
-    )(queries, keys, values, span_ids.reshape(wave, 1, group * tokens), res, gain.reshape(1, width), routes, gates, wg, wu, wd)
+    )(queries, keys, values, span_ids.reshape(wave, 1, group * tokens), res, gain.reshape(1, width), routes.T, gates.T, wg, wu, wd)
 
 
 def solution(mesh):

time: 78.5 us -> 68.9 us (0.88)
  local copies, waits for them, and re-layouts: 8.48 us -> 1.67 us
  Pallas kernels: 69.6 us -> 67 us
    unnamed x23 -> x1, local copies, waits for them, and re-layouts: 8.48 us -> 1.67 us
    pallas_call x1, Pallas kernels: 69.6 us -> 67 us  [layer(): pl.pallas_call(functools.partial(moe_kernel, group), out_shape=jax.ShapeD...]
where the time goes in v4:
time: 68.9 us; the launch traced here: 68.7 us
  Pallas kernels  67 us (97%)
  local copies, waits for them, and re-layouts  1.67 us (2%)
    pallas_call x1, Pallas kernels, layer(): pl.pallas_call(functools.partial(moe_kernel, group), out_shape=jax.ShapeD...  67 us
    unnamed x1, local copies, waits for them, and re-layouts  1.67 us

profile of v4, /device:TPU:0, one launch (start us, length us, event | category | flops | bytes accessed | tf_op | source)
XLA Modules:
  0.0 68.7 jit_solution(2840668193718881732)
XLA Ops:
  0.0 67.0 %shard_map.109 = bf16[32,4096]{1,0:T(8,128)(2,1)} custom-call(bf16[1024,128]{1,0:T(8,128)(2,1)} %queries_hbm.1, bf16[32,256]{1,0:T(8,128)(2,1)} %keys_hbm.1, bf16[32,256]{1,0:T(8,128)(2,1)} %values_hbm.1, s32[4,1,256]{2,1,0:T(1,128)} %bitcast.5, bf16[32,4096]{1,0:T(8,128)(2,1)} %res_hbm.1, f32[1,4096]{1,0:T(1,128)} %bitcast.4, s32[8,32]{1,0:T(8,128)} %bitcast.6, ...), custom_call_target="tpu_custom_call" | custom-call | tf_op jit(solution)/shard_map/pallas_call | solution.py:287
  67.0 1.7 %copy.13 = bf16[32,4096]{1,0:T(8,128)(2,1)} copy(bf16[32,4096]{1,0:T(8,128)(2,1)} %shard_map.109) | data formatting | bytes 524288

commit v5 on v4

--- a/solution.py
+++ b/solution.py
@@ -154,27 +154,29 @@
         joined = heads[0] if len(heads) == 1 else jnp.concatenate(heads, axis=0)
         return joined.T.astype(BF16).reshape(group, tokens, query.shape[1])
 
-    def spread(rz):
-        if rz:
-            arrived(att_in.at[rz], az_recv.at[rz])
-        target = att_buf.at[plane ^ rz, mine]
+    later = wave // 2
+
+    def spread(part_at, first):
+        block = pl.ds(first, later)
+        for rz in range(first, first + later):
+            if rz:
+                arrived(att_in.at[rz], az_recv.at[rz])
         for r in range(1, group):
-            go(remote(att_in.at[rz, mine ^ r], target, a_send.at[rz, r], a_recv.at[rz, r], within(r)))
-        att_buf[plane ^ rz, mine] = att_in[rz, mine]
+            go(remote(att_in.at[block, mine ^ r], att_buf.at[block, mine],
+                      a_send.at[part_at, r], a_recv.at[part_at, r], within(r)))
+        att_buf[block, mine] = att_in[block, mine]
 
     for rz in range(wave - 1, 0, -1):
         att_own[rz] = attend(plane ^ rz)
         go(remote(att_own.at[rz], att_in.at[rz], az_send.at[rz], az_recv.at[rz], across(rz)))
-        if rz < wave - 2:
-            spread(rz + 2)
+    spread(0, later)
     att_in[0] = attend(plane)
-    for rz in range(min(2, wave - 1), -1, -1):
-        spread(rz)
-    for rz in range(wave):
+    spread(1, 0)
+    for part_at, first in ((0, later), (1, 0)):
         for r in range(1, group):
-            arrived(att_buf.at[plane ^ rz, mine ^ r], a_recv.at[rz, r])
+            arrived(att_buf.at[pl.ds(first, later), mine ^ r], a_recv.at[part_at, r])
     att = jnp.concatenate(
-        [att_buf[index // group, index % group] for index in range(wave * group)], axis=1
+        [att_buf[plane ^ (index // group), index % group] for index in range(wave * group)], axis=1
     )
     for name in ("res", "gain"):
         fetched[name].wait()
@@ -198,10 +200,9 @@
 
     def fold(k):
         arrived(core_buf.at[k], c_recv.at[k])
-        total = part[2 * k].astype(F32) + core_buf[k].astype(F32)
-        sums[k] = total.astype(BF16)
-        if k:
-            go(remote(sums.at[k], plane_buf.at[k], p_send.at[k], p_recv.at[k], within(2 * k)))
+        for rz in range(wave - 1, -1, -1):
+            sums[k, rz] = (part[2 * k, rz].astype(F32) + core_buf[k, rz].astype(F32)).astype(BF16)
+            go(remote(sums.at[k, rz], plane_buf.at[k, rz], p_send.at[k, rz], p_recv.at[k, rz], within(2 * k)))
 
     def landed(r, rz):
         arrived(x_buf.at[r, rz], x_recv.at[r, rz])
@@ -231,26 +232,27 @@
         pre = (left + right).reshape(2 * wave * capacity, 2 * hidden_here)
         gate_pre, up_pre = pre[:, :hidden_here], pre[:, hidden_here:]
         hidden = (gate_pre / (1.0 + jnp.exp(-gate_pre)) * up_pre).astype(BF16)
-        piece = jnp.dot(hidden, wd_v[...], preferred_element_type=F32).astype(BF16)
-        part[r] = piece[:wave * capacity]
-        part[r + 1] = piece[wave * capacity:]
+        piece = jnp.dot(hidden, wd_v[...], preferred_element_type=F32)
+        for number in range(2 * wave):
+            block = piece[number * capacity:(number + 1) * capacity]
+            block = jnp.concatenate([block[:, :half], block[:, half:]], axis=0).astype(BF16)
+            part[r + number // wave, number % wave] = block
         go(remote(part.at[r + 1], core_buf.at[k], c_send.at[k], c_recv.at[k], within(1)))
-        if k:
+        if k > 1:
             fold(k - 1)
     fold(pairs - 1)
 
-    total = sums[0].astype(F32)
-    for k in range(1, pairs):
-        arrived(plane_buf.at[k], p_recv.at[k])
-        total = total + plane_buf[k].astype(F32)
-    for rz in range(wave):
-        block = total[rz * capacity:(rz + 1) * capacity]
-        block = jnp.concatenate([block[:, :half], block[:, half:]], axis=0).astype(BF16)
+    arrived(core_buf.at[0], c_recv.at[0])
+    for rz in range(wave - 1, -1, -1):
+        total = part[0, rz].astype(F32) + core_buf[0, rz].astype(F32)
+        for k in range(1, pairs):
+            arrived(plane_buf.at[k, rz], p_recv.at[k, rz])
+            total = total + plane_buf[k, rz].astype(F32)
         if rz:
-            final[rz] = block
+            final[rz] = total.astype(BF16)
             go(remote(final.at[rz], back.at[plane], b_send.at[rz], b_recv.at[rz], across(rz)))
         else:
-            back[plane] = block
+            back[plane] = total.astype(BF16)
     for rz in range(1, wave):
         arrived(back.at[plane ^ rz], b_recv.at[rz])
 
@@ -283,7 +285,6 @@
     vmem = pl.BlockSpec(memory_space=pltpu.VMEM)
     hbm = pl.BlockSpec(memory_space=pl.ANY)
     dma = pltpu.SemaphoreType.DMA
-    rows = wave * capacity
     return pl.pallas_call(
         functools.partial(moe_kernel, group),
         out_shape=jax.ShapeDtypeStruct((tokens, width), BF16),
@@ -311,14 +312,14 @@
             pltpu.VMEM((wd.shape[0], width), BF16),
             pltpu.VMEM((wave, 2 * capacity, half), BF16),
             pltpu.VMEM((group, wave, 2 * capacity, half), BF16),
-            pltpu.VMEM((group, rows, width), BF16),
-            pltpu.VMEM((pairs, rows, width), BF16),
-            pltpu.VMEM((pairs, rows, width), BF16),
-            pltpu.VMEM((pairs, rows, width), BF16),
+            pltpu.VMEM((group, wave, 2 * capacity, half), BF16),
+            pltpu.VMEM((pairs, wave, 2 * capacity, half), BF16),
+            pltpu.VMEM((pairs, wave, 2 * capacity, half), BF16),
+            pltpu.VMEM((pairs, wave, 2 * capacity, half), BF16),
             pltpu.VMEM((wave, 2 * capacity, half), BF16),
             pltpu.VMEM((wave, 2 * capacity, half), BF16),
             dma((3,)), dma((wave,)), dma((group, wave)), dma((group, wave)),
-            dma((pairs,)), dma((pairs,)), dma((pairs,)), dma((pairs,)), dma((wave,)), dma((wave,)),
+            dma((pairs,)), dma((pairs,)), dma((pairs, wave)), dma((pairs, wave)), dma((wave,)), dma((wave,)),
         ],
         compiler_params=pltpu.CompilerParams(
             collective_id=0, has_side_effects=True, vmem_limit_bytes=60 * 2**20

time: 68.9 us -> 64.7 us (0.939)
  Pallas kernels: 67 us -> 62.8 us
    pallas_call x1, Pallas kernels: 67 us -> 62.8 us  [layer(): pl.pallas_call(functools.partial(moe_kernel, group), out_shape=jax.ShapeD...]
where the time goes in v5:
time: 64.7 us; the launch traced here: 64.5 us
  Pallas kernels  62.8 us (97%)
  local copies, waits for them, and re-layouts  1.67 us (3%)
    pallas_call x1, Pallas kernels, layer(): pl.pallas_call(functools.partial(moe_kernel, group), out_shape=jax.ShapeD...  62.8 us
    unnamed x1, local copies, waits for them, and re-layouts  1.67 us

profile of v5, /device:TPU:0, one launch (start us, length us, event | category | flops | bytes accessed | tf_op | source)
XLA Modules:
  0.0 64.5 jit_solution(17689656069844813894)
XLA Ops:
  0.0 62.8 %shard_map.109 = bf16[32,4096]{1,0:T(8,128)(2,1)} custom-call(bf16[1024,128]{1,0:T(8,128)(2,1)} %queries_hbm.1, bf16[32,256]{1,0:T(8,128)(2,1)} %keys_hbm.1, bf16[32,256]{1,0:T(8,128)(2,1)} %values_hbm.1, s32[4,1,256]{2,1,0:T(1,128)} %bitcast.5, bf16[32,4096]{1,0:T(8,128)(2,1)} %res_hbm.1, f32[1,4096]{1,0:T(1,128)} %bitcast.4, s32[8,32]{1,0:T(8,128)} %bitcast.6, ...), custom_call_target="tpu_custom_call" | custom-call | tf_op jit(solution)/shard_map/pallas_call | solution.py:288
  62.8 1.7 %copy.13 = bf16[32,4096]{1,0:T(8,128)(2,1)} copy(bf16[32,4096]{1,0:T(8,128)(2,1)} %shard_map.109) | data formatting | bytes 524288
